TPU v7x, 128 devices: a whole 4x4x4 slice. The times are simulated.
128 devices in a mesh: img: 8 (over x, z_lo), txt: 16 (over y, z_hi, core).
Axes of the slice: x: 4, y: 4, z: 4 (z_hi: 2, z_lo: 2; z = z_hi * 2 + z_lo), core: 2. Of those that a mesh axis runs over, the one named last changes fastest.
Arguments:
- image: bfloat16 [20480, 1152], P(('img', 'txt')), may hold values from -6 to 6
- text: bfloat16 [20480, 1152], P('txt', 'img'), may hold values from -6 to 6
- pair_text: int32 [20480], P(('img', 'txt')), may hold values from 0 to 20479, each once
- log_scale: float32 [1], replicated, may hold values from 2.3 to 3
- bias: float32 [1], replicated, may hold values from -3 to -1
Outputs:
- grad_image: bfloat16 [20480, 1152], P(('img', 'txt'))
- grad_text: bfloat16 [20480, 1152], P('txt', 'img')
Inputs may be any that keep to these rules, and one draw needn't show every extreme that they name: `pair_text`: each text index is the match of exactly one image.
All inputs are finite; a program needn't handle non-finite values.
Results may differ from a plain program's by a relative error of at most 0.0034.
Values may be sent and summed in bfloat16 or wider, within the bound.
No kernel may reach another device: no remote copies, remote signals or barrier semaphores. Data moves between devices by JAX's collectives and lax.ppermute only.
A program may use at most 128 MiB of HBM per device.

v0:
```python
import jax
import jax.numpy as jnp
from jax import lax
from jax.sharding import PartitionSpec as P


def normalize(rows):
    values = rows.astype(jnp.float32)
    scale = jnp.sqrt(jnp.sum(values * values, axis=-1, keepdims=True) + 1e-06)
    return (values / scale, scale)


def local(image, text, pair_text, log_scale, bias):
    image_dir, image_norm = normalize(image)
    image_unit = image_dir.astype(jnp.bfloat16)
    unit_block, pair_block = (
        lax.all_gather(image_unit, "txt", axis=0, tiled=True),
        lax.all_gather(pair_text, "txt", axis=0, tiled=True),
    )
    text_block = lax.all_gather(text, "img", axis=1, tiled=True)
    text_dir, text_norm = normalize(text_block)
    text_unit = text_dir.astype(jnp.bfloat16)
    temper = jnp.exp(log_scale[0])
    shift = bias[0]
    width = text_unit.shape[1]
    text_rows = text_unit.shape[0]
    columns = lax.axis_index("txt") * text_rows + jnp.arange(text_rows, dtype=jnp.int32)
    count = lax.axis_size("txt") // 4
    blocks = unit_block.reshape(count, -1, width)
    pair_blocks = pair_block.reshape(count, -1)

    def tile(inputs):
        rows, pairs = inputs
        logits = (
            temper * jnp.einsum("rd,cd->rc", rows, text_unit, preferred_element_type=jnp.float32)
            + shift
        )
        positive = pairs[:, None] == columns[None, :]
        return (jax.nn.sigmoid(logits) - positive.astype(jnp.float32)).astype(jnp.bfloat16)

    weights = lax.map(tile, (blocks, pair_blocks))
    weight = weights.reshape(unit_block.shape[0], text_rows)
    image_back = lax.psum_scatter(
        temper * jnp.dot(weight, text_unit, preferred_element_type=jnp.float32),
        "txt",
        scatter_dimension=0,
        tiled=True,
    )
    grad_image = (
        image_back - image_dir * jnp.sum(image_dir * image_back, axis=-1, keepdims=True)
    ) / image_norm
    text_back = temper * jnp.einsum(
        "rc,rd->cd", weight, unit_block, preferred_element_type=jnp.float32
    )
    slice_width = text.shape[1]
    share = lax.psum_scatter(text_back, "img", scatter_dimension=1, tiled=True)
    offset = lax.axis_index("img") * slice_width
    dir_slice = lax.dynamic_slice_in_dim(text_dir, offset, slice_width, 1)
    dots = lax.psum(jnp.sum(dir_slice * share, axis=-1, keepdims=True), "img")
    grad_text = ((share - dir_slice * dots) / text_norm).astype(jnp.bfloat16)
    return (grad_image.astype(jnp.bfloat16), grad_text)


def solution(mesh):
    in_specs = (P(("img", "txt"), None), P("txt", "img"), P(("img", "txt")), P(), P())
    out_specs = (P(("img", "txt"), None), P("txt", "img"))
    return jax.shard_map(local, mesh=mesh, in_specs=in_specs, out_specs=out_specs, check_vma=False)
```

profile of v0, /device:TPU:6, one launch (start us, length us, event | category | flops | bytes accessed | tf_op | source)
XLA Modules:
  0.0 442.1 jit_solution(2673843407092207365)
XLA Ops:
  7.2 0.0 all-gather.5.cloned.1.call-start
  7.2 0.7 all-gather.5.cloned.1.call-update
  7.9 0.0 all-gather.3.cloned.1.call-start
  7.9 1.1 fusion.15
  9.1 1.9 fusion.16
  11.0 0.0 all-gather.3.cloned.1.call-update
  11.0 0.0 reduce-scatter.5.cloned.1.call-start
  11.1 1.3 dynamic-slice
  13.0 0.9 dynamic-update-slice
  13.9 71.8 %all-reduce = s32[2560]{0:T(1024)S(1)} all-reduce(s32[2560]{0:T(1024)S(1)} %dynamic-update-slice), channel_id=1, replica_groups=mesh['img'=8,'txt'=16] {'txt'}, use_global_device_ids=true, to_apply=%add | all-reduce | flops 2560 | bytes 20480
  86.4 0.0 all-gather.5.cloned.1.call-done
  86.4 2.5 fusion.14
  88.9 4.9 %convert_divide_fusion = (f32[1280,1152]{0,1:T(8,128)}, bf16[1280,1152]{0,1:T(8,128)(2,1)S(1)}) fusion(bf16[1280,1152]{0,1:T(8,128)(2,1)} %all-gather.5.cloned.1.call-done, f32[1280]{0:T(1024)S(1)} %add_sqrt_fusion), kind=kLoop, calls=%fused_computation.18 | loop fusion | flops 4423680 | bytes 11801600 | tf_op jit(solution)/shard_map/div | solution.py:10
  93.9 3.3 copy.7
  97.2 49.4 %all-gather.3.cloned.1.call-done = bf16[2560,1152]{1,0:T(8,128)(2,1)} async-done(((bf16[160,1152]{1,0:T(8,128)(2,1)}), bf16[2560,1152]{1,0:T(8,128)(2,1)}) %all-gather.3.cloned.1.call-update) | async-done | bytes 5898256 | tf_op jit(solution)/shard_map/all_gather | solution.py:17
  146.6 27.4 %while.11 = (s32[]{:T(128)}, bf16[4,640,1280]{2,1,0:T(8,128)(2,1)}, f32[]{:T(128)}, bf16[4,640,1152]{2,1,0:T(8,128)(2,1)}, bf16[1280,1152]{1,0:T(8,128)(2,1)}, /...) while((s32[]{:T(128)}, bf16[4,640,1280]{2,1,0:T(8,128)(2,1)}, f32[]{:T(128)}, ...), condition=%wide.region_3.4_spmd.clone, body=%wide.region_2.3_spmd.clone.sunk | while | flops 1894810880 | bytes 6082149 | solution.py:41
  146.6 6.9 %fusion.28 = bf16[4,640,1280]{2,1,0:T(8,128)(2,1)} fusion(bf16[4,640,1280]{2,1,0:T(8,128)(2,1)} %get-tuple-element.149, s32[]{:T(128)} %get-tuple-element.148, bf16[1280,1152]{1,0:T(8,128)(2,1)} %get-tuple-element.161, s32[1280]{0:T(1024)S(1)} %iota_add_fusion.2, f32[]{:T(128)} %get-tuple-element.162, f32[]{:T(128)} %get-tuple-element.159, ...), kind=kOutput, calls=%fused_computation.10.clone.1 | convolution fusion | flops 1894809600 | bytes 6071808 | tf_op jit(solution)/shard_map/while/body/eval_jaxpr/rd,cd->rc/dot_general | solution.py:35
  153.6 6.8 %fusion.28 = bf16[4,640,1280]{2,1,0:T(8,128)(2,1)} fusion(bf16[4,640,1280]{2,1,0:T(8,128)(2,1)} %get-tuple-element.149, s32[]{:T(128)} %get-tuple-element.148, bf16[1280,1152]{1,0:T(8,128)(2,1)} %get-tuple-element.161, s32[1280]{0:T(1024)S(1)} %iota_add_fusion.2, f32[]{:T(128)} %get-tuple-element.162, f32[]{:T(128)} %get-tuple-element.159, ...), kind=kOutput, calls=%fused_computation.10.clone.1 | convolution fusion | flops 1894809600 | bytes 6071808 | tf_op jit(solution)/shard_map/while/body/eval_jaxpr/rd,cd->rc/dot_general | solution.py:35
  160.4 6.8 %fusion.28 = bf16[4,640,1280]{2,1,0:T(8,128)(2,1)} fusion(bf16[4,640,1280]{2,1,0:T(8,128)(2,1)} %get-tuple-element.149, s32[]{:T(128)} %get-tuple-element.148, bf16[1280,1152]{1,0:T(8,128)(2,1)} %get-tuple-element.161, s32[1280]{0:T(1024)S(1)} %iota_add_fusion.2, f32[]{:T(128)} %get-tuple-element.162, f32[]{:T(128)} %get-tuple-element.159, ...), kind=kOutput, calls=%fused_computation.10.clone.1 | convolution fusion | flops 1894809600 | bytes 6071808 | tf_op jit(solution)/shard_map/while/body/eval_jaxpr/rd,cd->rc/dot_general | solution.py:35
  167.3 6.8 %fusion.28 = bf16[4,640,1280]{2,1,0:T(8,128)(2,1)} fusion(bf16[4,640,1280]{2,1,0:T(8,128)(2,1)} %get-tuple-element.149, s32[]{:T(128)} %get-tuple-element.148, bf16[1280,1152]{1,0:T(8,128)(2,1)} %get-tuple-element.161, s32[1280]{0:T(1024)S(1)} %iota_add_fusion.2, f32[]{:T(128)} %get-tuple-element.162, f32[]{:T(128)} %get-tuple-element.159, ...), kind=kOutput, calls=%fused_computation.10.clone.1 | convolution fusion | flops 1894809600 | bytes 6071808 | tf_op jit(solution)/shard_map/while/body/eval_jaxpr/rd,cd->rc/dot_general | solution.py:35
  174.1 13.1 %convolution_multiply_fusion.2 = f32[1280,1152]{0,1:T(8,128)} fusion(bf16[2560,1280]{1,0:T(8,128)(2,1)} %bitcast.25, bf16[2560,1152]{1,0:T(8,128)(2,1)} %bitcast.24, f32[]{:T(128)} %bitcast), kind=kOutput, calls=%fused_computation.17 | convolution fusion | flops 7551221760 | bytes 18350084 | tf_op jit(solution)/shard_map/rc,rd->cd/dot_general | solution.py:52
  187.2 0.0 reduce-scatter.5.cloned.1.call-update
  187.2 0.0 reduce-scatter.3.cloned.1.call-start
  187.2 13.4 %convolution_multiply_fusion.1 = f32[2560,1152]{1,0:T(8,128)} fusion(bf16[2560,1280]{1,0:T(8,128)(2,1)} %bitcast.26, bf16[1280,1152]{0,1:T(8,128)(2,1)S(1)} %get-tuple-element.89, f32[]{:T(128)} %bitcast), kind=kOutput, calls=%fused_computation.16 | convolution fusion | flops 7552696320 | bytes 21299204 | tf_op jit(solution)/shard_map/dot_general | solution.py:44
  200.7 0.0 reduce-scatter.3.cloned.1.call-update
  200.7 107.4 %reduce-scatter.5.cloned.1.call-done = f32[1280,144]{0,1:T(8,128)} async-done(((f32[1280,1152]{0,1:T(8,128)}), f32[1280,144]{0,1:T(8,128)}) %reduce-scatter.5.cloned.1.call-update) | async-done | bytes 737296 | tf_op jit(solution)/shard_map/reduce_scatter | solution.py:56
  308.1 1.4 multiply_reduce_fusion
  309.6 15.2 %psum.7 = f32[1280]{0:T(1024)S(1)} all-reduce(f32[1280]{0:T(1024)S(1)} %multiply_reduce_fusion), channel_id=1, replica_groups=mesh['img'=8,'txt'=16] {'img'}, use_global_device_ids=true, to_apply=%region_8.9 | all-reduce | flops 1280 | bytes 10240 | tf_op jit(solution)/shard_map/psum | solution.py:59
  324.8 2.4 divide_convert_fusion
  327.2 105.0 %reduce-scatter.3.cloned.1.call-done = f32[160,1152]{1,0:T(8,128)} async-done(((f32[2560,1152]{1,0:T(8,128)}), f32[160,1152]{1,0:T(8,128)}) %reduce-scatter.3.cloned.1.call-update) | async-done | bytes 737296 | tf_op jit(solution)/shard_map/reduce_scatter | solution.py:43
  432.1 1.4 multiply_reduce_fusion.1
  433.5 2.1 divide_convert_fusion.1
  (15 shorter events, 0.1 us)
Async XLA Ops:
  7.2 79.3 %all-gather.5.cloned.1.call-start = ((), (), s32[]{:S(2)}) async-start(), calls=%async_computation.3 | async-start | bytes 3317760 | tf_op jit(solution)/shard_map/all_gather | solution.py:20
  7.9 138.7 %all-gather.3.cloned.1.call-start = ((), (), s32[]{:S(2)}) async-start(), calls=%async_computation.2 | async-start | bytes 6266880 | tf_op jit(solution)/shard_map/all_gather | solution.py:17
  11.0 297.1 %reduce-scatter.5.cloned.1.call-start = ((), (), s32[]{:S(2)}) async-start(), calls=%async_computation.5 | async-start | bytes 6635520 | tf_op jit(solution)/shard_map/reduce_scatter | solution.py:56
  187.2 245.0 %reduce-scatter.3.cloned.1.call-start = ((), (), s32[]{:S(2)}) async-start(), calls=%async_computation.4 | async-start | bytes 12533760 | tf_op jit(solution)/shard_map/reduce_scatter | solution.py:43
  200.7 231.5 %copy-start = (bf16[160,1152]{1,0:T(8,128)(2,1)S(1)}, bf16[160,1152]{1,0:T(8,128)(2,1)}, u32[]{:S(2)}) copy-start(bf16[160,1152]{1,0:T(8,128)(2,1)} %param.7) | copy-start | bytes 1105924
Sparse Core Ops, SparseCore 0:
  9.6 69.9 all-gather.4
  82.6 63.9 all-gather.2
  187.3 120.7 reduce-scatter.4
  313.1 119.0 reduce-scatter.2
where the time goes:
time: 443 us; the launch traced here: 442 us
  waiting for transfers between devices  263 us (59%)
  blocking collectives  87 us (20%)
  matrix products  53.8 us (12%)
  other arithmetic  17.7 us (4%)
  between operations  15.2 us (3%)
  local copies, waits for them, and re-layouts  5.64 us (1%)
    reduce_scatter x1, waiting for transfers between devices, local(): share = lax.psum_scatter(text_back, 'img', scatter_dimension=1, tiled=True)  107 us
    reduce_scatter x1, waiting for transfers between devices, local(): lax.psum_scatter(temper * jnp.dot(weight, text_unit, preferred_element_ty...  105 us
    unnamed x1, blocking collectives  71.8 us
    all_gather x1, waiting for transfers between devices, local(): lax.all_gather(image_unit, 'txt', axis=0, tiled=True)  49.4 us
    dot_general x4, matrix products, tile(): jnp.einsum('rd,cd->rc', rows, text_unit, preferred_element_type=jnp.float32)  27.3 us
    psum x1, blocking collectives, local(): dots = lax.psum(jnp.sum(dir_slice * share, axis=-1, keepdims=True), 'img')  15.2 us
    dot_general x1, matrix products, local(): jnp.dot(weight, text_unit, preferred_element_type=jnp.float32)  13.4 us
    dot_general x1, matrix products, local(): jnp.einsum('rc,rd->cd', weight, unit_block, preferred_element_type=jnp.fl...  13.1 us
  transfers between devices with their start and end apart: 4, of which 3 were waited for; matrix products, arithmetic and copies ran while one was open for 8% of the time, Pallas kernels for 0%

commit v1 on v0

v1 whole, which is shorter than its diff:
```python
import jax
import jax.numpy as jnp
from jax import lax
from jax.experimental import pallas as pl
from jax.experimental.pallas import tpu as pltpu
from jax.sharding import PartitionSpec as P

F32 = jnp.float32
BF16 = jnp.bfloat16
VMEM = pl.BlockSpec(memory_space=pltpu.VMEM)
SMEM = pl.BlockSpec(memory_space=pltpu.SMEM)
LOG2E = 1.4426950408889634
AXES = ("img", "txt")
NN = (((1,), (0,)), ((), ()))
NT = (((1,), (1,)), ((), ()))
TN = (((0,), (0,)), ((), ()))
STEPS = (0, -1, 1, 2)
TAIL = 16


def params(mib):
    return pltpu.CompilerParams(vmem_limit_bytes=mib * 2**20)


def cost(flops, size):
    return pl.CostEstimate(flops=flops, bytes_accessed=size, transcendentals=0)


def moves():
    def perm(f):
        pairs = []
        for x in range(4):
            for y in range(4):
                for hi in range(2):
                    for lo in range(2):
                        for c in range(2):
                            a = (x, y, hi, lo, c)
                            number = lambda x, y, hi, lo, c: (x * 2 + lo) * 16 + (y * 2 + hi) * 2 + c
                            pairs.append((number(*a), number(*f(*a))))
        return pairs

    out = {}
    for s in (1, -1, 2):
        out["y", s] = perm(lambda x, y, hi, lo, c: (x, (y + s) % 4, hi, lo, c))
        out["x", s] = perm(lambda x, y, hi, lo, c: ((x + s) % 4, y, hi, lo, c))
    out["hi"] = perm(lambda x, y, hi, lo, c: (x, y, 1 - hi, lo, c))
    out["lo"] = perm(lambda x, y, hi, lo, c: (x, y, hi, 1 - lo, c))
    out["core"] = perm(lambda x, y, hi, lo, c: (x, y, hi, lo, 1 - c))
    return out


MOVES = moves()


def send(value, move):
    return lax.ppermute(value, AXES, MOVES[move])


def after(value, *others):
    return lax.optimization_barrier((value, *others))[0]


def split3(value, rounded=lambda v: v.astype(BF16).astype(F32)):
    high = rounded(value)
    middle = rounded(value - high)
    return high, middle, rounded(value - high - middle)


def unit_kernel(image, pairs, out, inverse):
    value = image[...].astype(F32)
    scale = 1.0 / jnp.sqrt(jnp.sum(value * value, axis=1, keepdims=True) + 1e-06)
    inverse[...] = scale
    unit = (value * scale).astype(BF16)
    rows, width = unit.shape
    half = rows // 2
    out[:half, :] = unit[:half]
    out[half + TAIL :, :] = unit[half:]
    index = pairs[...]
    kind = lax.broadcasted_iota(jnp.int32, (TAIL, width), 0)
    part = jnp.where(kind == 0, index >> 8, jnp.where(kind == 1, index & 255, 0))
    out[half : half + TAIL, :] = part.astype(F32).astype(BF16)


def image_units(image, pairs):
    rows, width = image.shape
    pairs = jnp.pad(pairs[None], ((0, 0), (0, width - rows)))
    return pl.pallas_call(
        unit_kernel,
        out_shape=[
            jax.ShapeDtypeStruct((rows + TAIL, width), BF16),
            jax.ShapeDtypeStruct((rows, 1), F32),
        ],
        in_specs=[VMEM] * 2,
        out_specs=[VMEM] * 2,
        compiler_params=params(8),
        cost_estimate=cost(0, 4 * rows * width),
        name="image_units",
    )(image, pairs)


def text_kernel(place, *refs):
    pieces, (unit, raw, inverse) = refs[:-3], refs[-3:]
    total = None
    for piece in pieces:
        value = piece[...].astype(F32)
        part = jnp.sum(value * value, axis=0, keepdims=True)
        total = part if total is None else total + part
    scale = 1.0 / jnp.sqrt(total + 1e-06)
    inverse[...] = scale
    depth = unit.shape[0] // 8
    block = 0
    for piece in pieces:
        for start in range(0, piece.shape[0], depth):
            rows = pl.ds(pl.multiple_of(place[block] * depth, 16), depth)
            value = piece[start : start + depth, :]
            raw[rows, :] = value
            unit[rows, :] = (value.astype(F32) * scale).astype(BF16)
            block += 1


def text_units(place, pieces, depth):
    width = pieces[0].shape[1]
    whole = jax.ShapeDtypeStruct((8 * depth, width), BF16)
    return pl.pallas_call(
        text_kernel,
        out_shape=[whole, whole, jax.ShapeDtypeStruct((1, width), F32)],
        in_specs=[SMEM] + [VMEM] * len(pieces),
        out_specs=[VMEM] * 3,
        compiler_params=params(12),
        cost_estimate=cost(0, 32 * depth * width),
        name="text_units",
    )(place, *pieces)


def weight_kernel(rows, scalars, first_text, *refs):
    pieces, text, (image, weight, other) = refs[:-4], refs[-4], refs[-3:]
    half = rows // 2
    slope, shift = scalars[0], scalars[1]
    columns = text.shape[1]
    eye = lax.broadcasted_iota(jnp.int32, (rows, rows), 0) == lax.broadcasted_iota(
        jnp.int32, (rows, rows), 1
    )
    names = (lax.broadcasted_iota(jnp.int32, (rows, columns), 1) + first_text[0]).astype(F32)
    block = 0
    for piece in pieces:
        for start in range(0, piece.shape[0], rows + TAIL):
            at = block * rows
            image[at : at + half, :] = piece[start : start + half, :]
            image[at + half : at + rows, :] = piece[start + half + TAIL : start + rows + TAIL, :]
            tail = piece[start + half : start + half + TAIL, :rows].astype(F32)
            product = lax.dot_general(
                image[at : at + rows, :], text[...], NN, preferred_element_type=F32
            )
            chance = 1.0 / (1.0 + jnp.exp2(product * slope + shift))
            match = jnp.sum(
                jnp.where(eye, tail[0:1] * 256.0 + tail[1:2], 0.0), axis=1, keepdims=True
            )
            value = (chance - jnp.where(match == names, 1.0, 0.0)).astype(BF16)
            weight[at : at + rows, :] = value
            if block >= 4:
                at -= 4 * rows
                other[at : at + rows, :] = value
            block += 1


def weights(scalars, first_text, pieces, rows, text):
    width, columns = text.shape
    count = 8 * rows
    return pl.pallas_call(
        lambda *refs: weight_kernel(rows, *refs),
        out_shape=[
            jax.ShapeDtypeStruct((count, width), BF16),
            jax.ShapeDtypeStruct((count, columns), BF16),
            jax.ShapeDtypeStruct((count // 2, columns), BF16),
        ],
        in_specs=[SMEM, SMEM] + [VMEM] * (len(pieces) + 1),
        out_specs=[VMEM] * 3,
        compiler_params=params(12),
        cost_estimate=cost(2 * count * width * columns, 2 * count * (width + columns)),
        name="weights",
    )(scalars, first_text, *pieces, text)


def text_back_kernel(place, image_a, weight_a, image_b, weight_b, raw, *refs):
    outs, back = refs[:4], refs[4]
    width, columns = back.shape
    block = 384
    dots = jnp.zeros((1, columns), F32)
    for f in range(0, width, block):
        part = lax.dot_general(
            image_a[:, f : f + block], weight_a[...], TN, preferred_element_type=F32
        ) + lax.dot_general(
            image_b[:, f : f + block], weight_b[...], TN, preferred_element_type=F32
        )
        back[f : f + block, :] = part
        dots += jnp.sum(part * raw[f : f + block, :].astype(F32), axis=0, keepdims=True)
    tail = split3(dots)
    empty = jnp.zeros((1, columns), F32)
    depth = width // 4
    for i in range(4):
        start = pl.multiple_of(place[2 * i] // 2 * depth, 8)
        out = outs[i]
        out[:depth, :] = back[pl.ds(start, depth), :].astype(out.dtype)
        spread = [empty] * 3 * i + list(tail) + [empty] * (TAIL - 3 * i - 3)
        out[depth:, :] = jnp.concatenate(spread, 0).astype(out.dtype)


def text_terms(place, image_a, weight_a, image_b, weight_b, raw):
    count, width = image_a.shape
    columns = weight_a.shape[1]
    shape = (width // 4 + TAIL, columns)
    return pl.pallas_call(
        text_back_kernel,
        out_shape=[jax.ShapeDtypeStruct(shape, F32)] + [jax.ShapeDtypeStruct(shape, BF16)] * 3,
        in_specs=[SMEM] + [VMEM] * 5,
        out_specs=[VMEM] * 4,
        scratch_shapes=[pltpu.VMEM((width, columns), F32)],
        compiler_params=params(16),
        cost_estimate=cost(4 * count * width * columns, 4 * count * columns),
        name="text_terms",
    )(place, image_a, weight_a, image_b, weight_b, raw)


def image_back_kernel(rows, own_a, got_a, own_b, got_b, text, text_got, *outs):
    for h, (own, got) in enumerate(((own_a, got_a), (own_b, got_b))):
        back = lax.dot_general(
            own[: 4 * rows, :], text[...], NT, preferred_element_type=F32
        ) + lax.dot_general(got[...], text_got[...], NT, preferred_element_type=F32)
        for k in range(4):
            out = outs[k]
            out[h * rows : (h + 1) * rows, :] = back[k * rows : (k + 1) * rows].astype(out.dtype)


def image_terms(rows, own_a, got_a, own_b, got_b, text, text_got):
    width, columns = text.shape
    kinds = [F32, BF16, BF16, BF16]
    return pl.pallas_call(
        lambda *refs: image_back_kernel(rows, *refs),
        out_shape=[jax.ShapeDtypeStruct((2 * rows, width), kind) for kind in kinds],
        in_specs=[VMEM] * 6,
        out_specs=[VMEM] * 4,
        compiler_params=params(16),
        cost_estimate=cost(32 * rows * width * columns, 8 * width * columns),
        name="image_terms",
    )(own_a, got_a, own_b, got_b, text, text_got)


def ring_sum(parts, axis):
    far = [send(part, (axis, s)) for s, part in zip(STEPS[1:], parts[1:])]
    return parts[0] + sum(part.astype(F32) for part in far)


def text_final_kernel(temper, low, total, given, raw, inverse, out):
    depth = raw.shape[0]
    scale = inverse[...]
    keep = total[pl.ds(pl.multiple_of(low[0] * depth, 8), depth), :]
    back = keep + given[:depth, :].astype(F32)
    tails = total[2 * depth :, :] + given[depth:, :].astype(F32)
    dots = jnp.sum(tails, axis=0, keepdims=True) * scale
    unit = raw[...].astype(F32) * scale
    out[...] = (temper[0] * (back - unit * dots) * scale).astype(BF16)


def text_final(temper, low, total, given, raw, inverse):
    return pl.pallas_call(
        text_final_kernel,
        out_shape=jax.ShapeDtypeStruct(raw.shape, BF16),
        in_specs=[SMEM, SMEM] + [VMEM] * 4,
        out_specs=VMEM,
        compiler_params=params(8),
        cost_estimate=cost(0, 4 * raw.size),
        name="text_final",
    )(temper, low, total, given, raw, inverse)


def gather_ring(piece, axis):
    return [piece] + [send(piece, (axis, -s if s < 2 else s)) for s in STEPS[1:]]


def local(image, text, pair_text, log_scale, bias):
    img, txt = lax.axis_index("img"), lax.axis_index("txt")
    x, lo = img // 2, img % 2
    place = jnp.stack([(x + s + 4) % 4 * 2 + (lo + h) % 2 for s in STEPS for h in range(2)])
    temper = jnp.exp(log_scale[0])
    scalars = jnp.stack([-LOG2E * temper, -LOG2E * bias[0]])
    first_text = (txt * text.shape[0])[None]
    depth, rows = text.shape[1], image.shape[0]

    own_text = text.T
    text_lo = send(own_text, "lo")
    unit, image_inverse = image_units(image, pair_text)
    near = [unit, send(unit, ("y", 1)), send(unit, ("y", -1))]
    near.append(send(after(unit, *near[1:]), ("y", 2)))
    text_pieces = gather_ring(jnp.concatenate([own_text, text_lo], 0), "x")
    unit_hi = send(after(unit, text_lo), "hi")
    unit_hi = after(unit_hi, near[3])
    partner = [unit_hi, send(unit_hi, ("y", 1)), send(unit_hi, ("y", -1))]
    partner.append(send(after(unit_hi, *partner[1:]), ("y", 2)))
    near.append(send(jnp.concatenate(near, 0), "core"))
    partner.append(send(jnp.concatenate(partner, 0), "core"))

    text_unit, text_raw, text_inverse = text_units(place, text_pieces, depth)
    text_got = send(text_unit, "core")
    image_a, weight_a, other_a = weights(scalars, first_text, near, rows, text_unit)
    got_a = send(other_a, "core")
    image_b, weight_b, other_b = weights(scalars, first_text, partner, rows, text_unit)
    got_b = send(other_b, "core")
    text_parts = text_terms(place, image_a, weight_a, image_b, weight_b, text_raw)
    got_b, *text_parts = lax.optimization_barrier((got_b, *text_parts))
    image_parts = image_terms(rows, weight_a, got_a, weight_b, got_b, text_unit, text_got)

    image_back = ring_sum(image_parts, "y")
    image_back = image_back[:rows] + send(image_back[rows:].astype(BF16), "hi").astype(F32)
    image_dir = image.astype(F32) * image_inverse
    dot = jnp.sum(image_dir * image_back, axis=-1, keepdims=True)
    grad_image = temper * (image_back - image_dir * dot) * image_inverse

    total = ring_sum(text_parts, "x")
    low_half, high_half, tail = total[:depth], total[depth : 2 * depth], total[2 * depth :]
    give = jnp.where(lo == 0, high_half, low_half)
    given = send(jnp.concatenate([give, tail], 0).astype(BF16), "lo")
    grad_text = text_final(temper[None], lo[None], total, given, own_text, text_inverse).T
    return grad_image.astype(BF16), grad_text


def solution(mesh):
    in_specs = (P(("img", "txt"), None), P("txt", "img"), P(("img", "txt")), P(), P())
    out_specs = (P(("img", "txt"), None), P("txt", "img"))
    return jax.shard_map(local, mesh=mesh, in_specs=in_specs, out_specs=out_specs, check_vma=False)
```

time: 443 us -> 195 us (0.44)
  waiting for transfers between devices: 263 us -> 107 us
  blocking collectives: 87 us -> 0 us
  matrix products: 53.8 us -> 0 us
  Pallas kernels: 0 us -> 41.3 us
  starting transfers between devices: 0.16 us -> 28.5 us
  between operations: 15.2 us -> 2.17 us
  other arithmetic: 17.7 us -> 8.06 us
    reduce_scatter x2 -> x0, waiting for transfers between devices: 212 us -> none  [the longest x1 107 us: local(): share = lax.psum_scatter(text_back, 'img', scatter_dimension=1, tiled=True)]
    ppermute x0 -> x24, waiting for transfers between devices: none -> 107 us  [send(): return lax.ppermute(value, AXES, MOVES[move])]
    unnamed x1 -> x0, blocking collectives: 71.8 us -> none
    dot_general x6 -> x0, matrix products: 53.8 us -> none  [the longest x4 27.3 us: tile(): jnp.einsum('rd,cd->rc', rows, text_unit, preferred_element_type=jnp.float32)]
    all_gather x2 -> x0, waiting for transfers between devices: 49.4 us -> none  [the longest x1 49.4 us: local(): lax.all_gather(image_unit, 'txt', axis=0, tiled=True)]
    pallas_call x0 -> x7, Pallas kernels: none -> 41.3 us  [the longest x2 14.3 us: weights(): pl.pallas_call(lambda *refs: weight_kernel(rows, *refs), out_shape=[jax.S...]
    ppermute x0 -> x24, starting transfers between devices: none -> 28.5 us  [send(): return lax.ppermute(value, AXES, MOVES[move])]
    psum x1 -> x0, blocking collectives: 15.2 us -> none  [local(): dots = lax.psum(jnp.sum(dir_slice * share, axis=-1, keepdims=True), 'img')]
  transfers between devices with their start and end apart: 4 -> 24, of which waited for: 3 -> 14; matrix products, arithmetic and copies ran while one was open for 8% -> 4% of each run, Pallas kernels for 0% -> 14%
where the time goes in v1:
time: 195 us; the launch traced here: 194 us
  waiting for transfers between devices  107 us (55%)
  Pallas kernels  41.3 us (21%)
  starting transfers between devices  28.5 us (15%)
  other arithmetic  8.06 us (4%)
  local copies, waits for them, and re-layouts  7.51 us (4%)
  between operations  2.17 us (1%)
    ppermute x24, waiting for transfers between devices, send(): return lax.ppermute(value, AXES, MOVES[move])  107 us
    ppermute x24, starting transfers between devices, send(): return lax.ppermute(value, AXES, MOVES[move])  28.5 us
    pallas_call x2, Pallas kernels, weights(): pl.pallas_call(lambda *refs: weight_kernel(rows, *refs), out_shape=[jax.S...  14.3 us
    pallas_call x1, Pallas kernels, image_terms(): pl.pallas_call(lambda *refs: image_back_kernel(rows, *refs), out_shape=[j...  12.5 us
    pallas_call x1, Pallas kernels, text_terms(): pl.pallas_call(text_back_kernel, out_shape=[jax.ShapeDtypeStruct(shape, F...  10 us
    unnamed x42, local copies, waits for them, and re-layouts  6.69 us
  transfers between devices with their start and end apart: 24, of which 14 were waited for; matrix products, arithmetic and copies ran while one was open for 4% of the time, Pallas kernels for 14%

profile of v1, /device:TPU:6, one launch (start us, length us, event | category | flops | bytes accessed | tf_op | source)
XLA Modules:
  0.0 194.2 jit_solution(13801927453726974958)
XLA Ops:
  2.5 1.6 collective-permute-start
  4.1 1.7 collective-permute-start.1
  5.8 1.9 collective-permute-start.4
  7.7 8.4 %collective-permute-done.4 = bf16[144,1280]{1,0:T(8,128)(2,1)S(1)} collective-permute-done((bf16[144,1280]{1,0:T(8,128)(2,1)}, bf16[144,1280]{1,0:T(8,128)(2,1)S(1)}, u32[]{:S(2)}, u32[]{:S(2)}) %collective-permute-start.4) | collective-permute-done | bytes 368672 | tf_op jit(solution)/shard_map/ppermute | solution.py:56
  16.2 3.6 %collective-permute-start.9 = (bf16[176,1152]{1,0:T(8,128)(2,1)S(1)}, bf16[176,1152]{1,0:T(8,128)(2,1)S(1)}, u32[]{:S(2)}, u32[]{:S(2)}) collective-permute-start(bf16[176,1152]{1,0:T(8,128)(2,1)S(1)} %get-tuple-element.35.refs_2_), channel_id=1, source_target_pairs={{0,2},{1,3},{16,18},{17,19},{2,0},{3,1},{18,16},{19,17},{4,6},{5,7... | collective-permute-start | bytes 1216520 | tf_op jit(solution)/shard_map/ppermute | solution.py:56
  19.8 1.9 collective-permute-start.2
  21.7 6.3 %collective-permute-done.9.refs_2_ = bf16[176,1152]{1,0:T(8,128)(2,1)S(1)} collective-permute-done((bf16[176,1152]{1,0:T(8,128)(2,1)S(1)}, bf16[176,1152]{1,0:T(8,128)(2,1)S(1)}, u32[]{:S(2)}, u32[]{:S(2)}) %collective-permute-start.9) | collective-permute-done | bytes 405536 | tf_op jit(solution)/shard_map/ppermute | solution.py:56
  28.1 2.8 %collective-permute-done.2.refs_5_ = bf16[176,1152]{1,0:T(8,128)(2,1)S(1)} collective-permute-done((bf16[176,1152]{1,0:T(8,128)(2,1)S(1)}, bf16[176,1152]{1,0:T(8,128)(2,1)S(1)}, u32[]{:S(2)}, u32[]{:S(2)}) %collective-permute-start.2) | collective-permute-done | bytes 405536 | tf_op jit(solution)/shard_map/ppermute | solution.py:56
  31.0 3.2 %collective-permute-start.11 = (bf16[176,1152]{1,0:T(8,128)(2,1)S(1)}, bf16[176,1152]{1,0:T(8,128)(2,1)S(1)}, u32[]{:S(2)}, u32[]{:S(2)}) collective-permute-start(bf16[176,1152]{1,0:T(8,128)(2,1)S(1)} %collective-permute-done.9.refs_2_), channel_id=1, source_target_pairs={{0,12},{1,13},{16,28},{17,29},{2,14},{3,15},{18,30},{19,31},{4,0},... | collective-permute-start | bytes 1216520 | tf_op jit(solution)/shard_map/ppermute | solution.py:56
  34.1 6.5 %collective-permute-done.10.refs_3_ = bf16[176,1152]{1,0:T(8,128)(2,1)S(1)} collective-permute-done((bf16[176,1152]{1,0:T(8,128)(2,1)S(1)}, bf16[176,1152]{1,0:T(8,128)(2,1)S(1)}, u32[]{:S(2)}, u32[]{:S(2)}) %collective-permute-start.10) | collective-permute-done | bytes 405536 | tf_op jit(solution)/shard_map/ppermute | solution.py:56
  40.7 1.5 collective-permute-start.12
  42.2 8.0 %collective-permute-done.12.refs_5_ = bf16[176,1152]{1,0:T(8,128)(2,1)S(1)} collective-permute-done((bf16[176,1152]{1,0:T(8,128)(2,1)S(1)}, bf16[176,1152]{1,0:T(8,128)(2,1)S(1)}, u32[]{:S(2)}, u32[]{:S(2)}) %collective-permute-start.12) | collective-permute-done | bytes 405536 | tf_op jit(solution)/shard_map/ppermute | solution.py:56
  52.2 1.5 collective-permute-start.6
  56.6 14.4 %collective-permute-done.5.refs_1_ = bf16[288,1280]{1,0:T(8,128)(2,1)S(1)} collective-permute-done((bf16[288,1280]{1,0:T(8,128)(2,1)S(1)}, bf16[288,1280]{1,0:T(8,128)(2,1)S(1)}, u32[]{:S(2)}, u32[]{:S(2)}) %collective-permute-start.5) | collective-permute-done | bytes 737312 | tf_op jit(solution)/shard_map/ppermute | solution.py:56
  71.0 16.8 %collective-permute-done.6.refs_2_ = bf16[288,1280]{1,0:T(8,128)(2,1)S(1)} collective-permute-done((bf16[288,1280]{1,0:T(8,128)(2,1)S(1)}, bf16[288,1280]{1,0:T(8,128)(2,1)S(1)}, u32[]{:S(2)}, u32[]{:S(2)}) %collective-permute-start.6) | collective-permute-done | bytes 737312 | tf_op jit(solution)/shard_map/ppermute | solution.py:56
  87.8 3.4 %text_units.1 = (bf16[1152,1280]{1,0:T(8,128)(2,1)}, bf16[1152,1280]{1,0:T(8,128)(2,1)S(1)}, f32[1,1280]{1,0:T(1,128)S(1)}) custom-call(s32[8]{0:T(128)S(1)} %stack.44.place, bf16[288,1280]{1,0:T(8,128)(2,1)S(1)} %pad_maximum_fusion.2.refs_0_, bf16[288,1280]{1,0:T(8,128)(2,1)S(1)} %collective-permute-done.5.refs_1_, ...), custom_call_target="tpu_custom_call" | custom-call | bytes 5898240 | tf_op jit(solution)/shard_map/text_units/pallas_call | solution.py:124
  91.2 1.6 copy-done.19
  98.3 7.2 %weights.3 = (bf16[1280,1152]{1,0:T(8,128)(2,1)S(1)}, bf16[1280,1280]{1,0:T(8,128)(2,1)S(1)}, bf16[640,1280]{1,0:T(8,128)(2,1)S(1)}) custom-call(f32[2]{0:T(128)S(1)} %pad_maximum_fusion.4.refs_0_, s32[1]{0:T(128)} %bitcast.2.refs_1_, bf16[176,1152]{1,0:T(8,128)(2,1)S(1)} %copy-done.12, bf16[176,1152]{1,0:T(8,128)(2,1)S(1)} %copy-done.14, ...), custom_call_target="tpu_custom_call" | custom-call | flops 3774873600 | bytes 6225920 | tf_op jit(solution)/shard_map/weights/pallas_call | solution.py:169
  106.3 7.1 %weights.2 = (bf16[1280,1152]{1,0:T(8,128)(2,1)S(1)}, bf16[1280,1280]{1,0:T(8,128)(2,1)S(1)}, bf16[640,1280]{1,0:T(8,128)(2,1)S(1)}) custom-call(f32[2]{0:T(128)S(1)} %pad_maximum_fusion.4.refs_0_, s32[1]{0:T(128)} %bitcast.2.refs_1_, bf16[176,1152]{1,0:T(8,128)(2,1)S(1)} %copy-done.4, bf16[176,1152]{1,0:T(8,128)(2,1)S(1)} %copy-done.6, ...), custom_call_target="tpu_custom_call" | custom-call | flops 3774873600 | bytes 6225920 | tf_op jit(solution)/shard_map/weights/pallas_call | solution.py:169
  113.7 10.0 %text_terms.1 = (f32[304,1280]{1,0:T(8,128)S(1)}, bf16[304,1280]{1,0:T(8,128)(2,1)}, bf16[304,1280]{1,0:T(8,128)(2,1)}, bf16[304,1280]{1,0:T(8,128)(2,1)}) custom-call(s32[8]{0:T(128)S(1)} %stack.44.place, bf16[1280,1152]{1,0:T(8,128)(2,1)S(1)} %get-tuple-element.40.image_a, bf16[1280,1280]{1,0:T(8,128)(2,1)S(1)} %get-tuple-element.33.weight_a.refs_0_, ...), custom_call_target="tpu_custom_call" | custom-call | flops 7549747200 | bytes 6553600 | tf_op jit(solution)/shard_map/text_terms/pallas_call | solution.py:212
  123.7 12.5 %image_terms.1 = (f32[320,1152]{1,0:T(8,128)S(1)}, bf16[320,1152]{1,0:T(8,128)(2,1)}, bf16[320,1152]{1,0:T(8,128)(2,1)}, bf16[320,1152]{1,0:T(8,128)(2,1)S(1)}) custom-call(bf16[1280,1280]{1,0:T(8,128)(2,1)S(1)} %get-tuple-element.33.weight_a.refs_0_, bf16[640,1280]{1,0:T(8,128)(2,1)S(1)} %collective-permute-done.8.refs_1_, ...), custom_call_target="tpu_custom_call" | custom-call | flops 7549747200 | bytes 11796480 | tf_op jit(solution)/shard_map/image_terms/pallas_call | solution.py:237
  136.2 1.4 collective-permute-start.18
  137.6 2.3 %collective-permute-start.17 = (bf16[320,1152]{1,0:T(8,128)(2,1)}, bf16[320,1152]{1,0:T(8,128)(2,1)}, u32[]{:S(2)}, u32[]{:S(2)}) collective-permute-start(bf16[320,1152]{1,0:T(8,128)(2,1)} %get-tuple-element.50), channel_id=1, source_target_pairs={{0,4},{1,5},{16,20},{17,21},{2,6},{3,7},{18,22},{19,23},{4,8},{5,9... | collective-permute-start | bytes 2211848 | tf_op jit(solution)/shard_map/ppermute | solution.py:56
  140.8 1.8 collective-permute-start.22
  142.9 14.2 %collective-permute-done.18 = bf16[320,1152]{1,0:T(8,128)(2,1)} collective-permute-done((bf16[320,1152]{1,0:T(8,128)(2,1)S(1)}, bf16[320,1152]{1,0:T(8,128)(2,1)}, u32[]{:S(2)}, u32[]{:S(2)}) %collective-permute-start.18) | collective-permute-done | bytes 737312 | tf_op jit(solution)/shard_map/ppermute | solution.py:56
  157.2 15.1 %collective-permute-done.17 = bf16[320,1152]{1,0:T(8,128)(2,1)} collective-permute-done((bf16[320,1152]{1,0:T(8,128)(2,1)}, bf16[320,1152]{1,0:T(8,128)(2,1)}, u32[]{:S(2)}, u32[]{:S(2)}) %collective-permute-start.17) | collective-permute-done | bytes 737312 | tf_op jit(solution)/shard_map/ppermute | solution.py:56
  172.6 1.9 add_add_fusion.1
  175.2 1.6 collective-permute-done.21
  176.7 1.5 collective-permute-done.20
  178.3 1.9 add_add_fusion.total
  181.3 6.3 %collective-permute-done.19 = bf16[160,1152]{1,0:T(8,128)(2,1)S(1)} collective-permute-done((bf16[160,1152]{1,0:T(8,128)(2,1)S(1)}, bf16[160,1152]{1,0:T(8,128)(2,1)S(1)}, u32[]{:S(2)}, u32[]{:S(2)}) %collective-permute-start.19) | collective-permute-done | bytes 368672 | tf_op jit(solution)/shard_map/ppermute | solution.py:56
  188.9 4.3 %collective-permute-done.23.given = bf16[160,1280]{1,0:T(8,128)(2,1)S(1)} collective-permute-done((bf16[160,1280]{1,0:T(8,128)(2,1)S(1)}, bf16[160,1280]{1,0:T(8,128)(2,1)S(1)}, u32[]{:S(2)}, u32[]{:S(2)}) %collective-permute-start.23) | collective-permute-done | bytes 409632 | tf_op jit(solution)/shard_map/ppermute | solution.py:56
  (80 shorter events, 17.5 us)
Async XLA Ops:
  2.5 52.7 %copy-start.3 = (bf16[176,1152]{1,0:T(8,128)(2,1)}, bf16[176,1152]{1,0:T(8,128)(2,1)S(1)}, u32[]{:S(2)}) copy-start(bf16[176,1152]{1,0:T(8,128)(2,1)S(1)} %get-tuple-element.35.refs_2_) | copy-start | bytes 1216516
  2.5 17.3 %collective-permute-start = (bf16[176,1152]{1,0:T(8,128)(2,1)S(1)}, bf16[176,1152]{1,0:T(8,128)(2,1)S(1)}, u32[]{:S(2)}, u32[]{:S(2)}) collective-permute-start(bf16[176,1152]{1,0:T(8,128)(2,1)S(1)} %get-tuple-element.35.refs_2_), channel_id=1, source_target_pairs={{0,4},{1,5},{16,20},{17,21},{2,6},{3,7},{18,22},{19,23},{4,8},{5,9... | collective-permute-start | bytes 1216520 | tf_op jit(solution)/shard_map/ppermute | solution.py:56
  4.1 15.7 %collective-permute-start.1 = (bf16[176,1152]{1,0:T(8,128)(2,1)S(1)}, bf16[176,1152]{1,0:T(8,128)(2,1)S(1)}, u32[]{:S(2)}, u32[]{:S(2)}) collective-permute-start(bf16[176,1152]{1,0:T(8,128)(2,1)S(1)} %get-tuple-element.35.refs_2_), channel_id=1, source_target_pairs={{0,12},{1,13},{16,28},{17,29},{2,14},{3,15},{18,30},{19,31},{4,0},... | collective-permute-start | bytes 1216520 | tf_op jit(solution)/shard_map/ppermute | solution.py:56
  5.8 45.8 %copy-start.2 = (bf16[1280,144]{0,1:T(8,128)(2,1)S(1)}, bf16[1280,144]{0,1:T(8,128)(2,1)}, u32[]{:S(2)}) copy-start(bf16[1280,144]{0,1:T(8,128)(2,1)} %param.6) | copy-start | bytes 1105924
  5.8 10.4 %collective-permute-start.4 = (bf16[144,1280]{1,0:T(8,128)(2,1)}, bf16[144,1280]{1,0:T(8,128)(2,1)S(1)}, u32[]{:S(2)}, u32[]{:S(2)}) collective-permute-start(bf16[144,1280]{1,0:T(8,128)(2,1)} %bitcast.15), channel_id=1, source_target_pairs={{0,16},{1,17},{16,0},{17,1},{2,18},{3,19},{18,2},{19,3},{4,20},{5,... | collective-permute-start | bytes 1105928 | tf_op jit(solution)/shard_map/ppermute | solution.py:56
  16.2 11.9 %collective-permute-start.9 = (bf16[176,1152]{1,0:T(8,128)(2,1)S(1)}, bf16[176,1152]{1,0:T(8,128)(2,1)S(1)}, u32[]{:S(2)}, u32[]{:S(2)}) collective-permute-start(bf16[176,1152]{1,0:T(8,128)(2,1)S(1)} %get-tuple-element.35.refs_2_), channel_id=1, source_target_pairs={{0,2},{1,3},{16,18},{17,19},{2,0},{3,1},{18,16},{19,17},{4,6},{5,7... | collective-permute-start | bytes 1216520 | tf_op jit(solution)/shard_map/ppermute | solution.py:56
  19.8 35.4 %copy-start.5 = (bf16[176,1152]{1,0:T(8,128)(2,1)}, bf16[176,1152]{1,0:T(8,128)(2,1)S(1)}, u32[]{:S(2)}) copy-start(bf16[176,1152]{1,0:T(8,128)(2,1)S(1)} %collective-permute-done.refs_3_) | copy-start | bytes 1216516
  19.8 35.4 %copy-start.7 = (bf16[176,1152]{1,0:T(8,128)(2,1)}, bf16[176,1152]{1,0:T(8,128)(2,1)S(1)}, u32[]{:S(2)}) copy-start(bf16[176,1152]{1,0:T(8,128)(2,1)S(1)} %collective-permute-done.1.refs_4_) | copy-start | bytes 1216516
  19.8 11.1 %collective-permute-start.2 = (bf16[176,1152]{1,0:T(8,128)(2,1)S(1)}, bf16[176,1152]{1,0:T(8,128)(2,1)S(1)}, u32[]{:S(2)}, u32[]{:S(2)}) collective-permute-start(bf16[176,1152]{1,0:T(8,128)(2,1)S(1)} %get-tuple-element.35.refs_2_), channel_id=1, source_target_pairs={{0,8},{1,9},{16,24},{17,25},{2,10},{3,11},{18,26},{19,27},{4,12},{... | collective-permute-start | bytes 1216520 | tf_op jit(solution)/shard_map/ppermute | solution.py:56
  28.1 23.4 %copy-start.11 = (bf16[176,1152]{1,0:T(8,128)(2,1)}, bf16[176,1152]{1,0:T(8,128)(2,1)S(1)}, u32[]{:S(2)}) copy-start(bf16[176,1152]{1,0:T(8,128)(2,1)S(1)} %collective-permute-done.9.refs_2_) | copy-start | bytes 1216516
  30.9 24.3 %copy-start.9 = (bf16[176,1152]{1,0:T(8,128)(2,1)}, bf16[176,1152]{1,0:T(8,128)(2,1)S(1)}, u32[]{:S(2)}) copy-start(bf16[176,1152]{1,0:T(8,128)(2,1)S(1)} %collective-permute-done.2.refs_5_) | copy-start | bytes 1216516
  30.9 9.8 %collective-permute-start.10 = (bf16[176,1152]{1,0:T(8,128)(2,1)S(1)}, bf16[176,1152]{1,0:T(8,128)(2,1)S(1)}, u32[]{:S(2)}, u32[]{:S(2)}) collective-permute-start(bf16[176,1152]{1,0:T(8,128)(2,1)S(1)} %collective-permute-done.9.refs_2_), channel_id=1, source_target_pairs={{0,4},{1,5},{16,20},{17,21},{2,6},{3,7},{18,22},{19,23},{4,8},{5,9... | collective-permute-start | bytes 1216520 | tf_op jit(solution)/shard_map/ppermute | solution.py:56
  31.0 9.7 %collective-permute-start.11 = (bf16[176,1152]{1,0:T(8,128)(2,1)S(1)}, bf16[176,1152]{1,0:T(8,128)(2,1)S(1)}, u32[]{:S(2)}, u32[]{:S(2)}) collective-permute-start(bf16[176,1152]{1,0:T(8,128)(2,1)S(1)} %collective-permute-done.9.refs_2_), channel_id=1, source_target_pairs={{0,12},{1,13},{16,28},{17,29},{2,14},{3,15},{18,30},{19,31},{4,0},... | collective-permute-start | bytes 1216520 | tf_op jit(solution)/shard_map/ppermute | solution.py:56
  40.7 10.8 %copy-start.13 = (bf16[176,1152]{1,0:T(8,128)(2,1)}, bf16[176,1152]{1,0:T(8,128)(2,1)S(1)}, u32[]{:S(2)}) copy-start(bf16[176,1152]{1,0:T(8,128)(2,1)S(1)} %collective-permute-done.10.refs_3_) | copy-start | bytes 1216516
  40.7 10.8 %copy-start.15 = (bf16[176,1152]{1,0:T(8,128)(2,1)}, bf16[176,1152]{1,0:T(8,128)(2,1)S(1)}, u32[]{:S(2)}) copy-start(bf16[176,1152]{1,0:T(8,128)(2,1)S(1)} %collective-permute-done.11.refs_4_) | copy-start | bytes 1216516
  40.7 9.5 %collective-permute-start.12 = (bf16[176,1152]{1,0:T(8,128)(2,1)S(1)}, bf16[176,1152]{1,0:T(8,128)(2,1)S(1)}, u32[]{:S(2)}, u32[]{:S(2)}) collective-permute-start(bf16[176,1152]{1,0:T(8,128)(2,1)S(1)} %collective-permute-done.9.refs_2_), channel_id=1, source_target_pairs={{0,8},{1,9},{16,24},{17,25},{2,10},{3,11},{18,26},{19,27},{4,12},{... | collective-permute-start | bytes 1216520 | tf_op jit(solution)/shard_map/ppermute | solution.py:56
  51.5 42.8 %collective-permute-start.13 = (bf16[704,1152]{1,0:T(8,128)(2,1)}, bf16[704,1152]{1,0:T(8,128)(2,1)}, u32[]{:S(2)}, u32[]{:S(2)}) collective-permute-start(bf16[704,1152]{1,0:T(8,128)(2,1)} %pad_maximum_fusion.1), channel_id=1, source_target_pairs={{0,1},{1,0},{16,17},{17,16},{2,3},{3,2},{18,19},{19,18},{4,5},{5,4... | collective-permute-start | bytes 4866056 | tf_op jit(solution)/shard_map/ppermute | solution.py:56
  51.7 19.4 %collective-permute-start.5 = (bf16[288,1280]{1,0:T(8,128)(2,1)S(1)}, bf16[288,1280]{1,0:T(8,128)(2,1)S(1)}, u32[]{:S(2)}, u32[]{:S(2)}) collective-permute-start(bf16[288,1280]{1,0:T(8,128)(2,1)S(1)} %pad_maximum_fusion.2.refs_0_), channel_id=1, source_target_pairs={{0,32},{1,33},{16,48},{17,49},{2,34},{3,35},{18,50},{19,51},{4,36}... | collective-permute-start | bytes 2211848 | tf_op jit(solution)/shard_map/ppermute | solution.py:56
  52.2 35.6 %collective-permute-start.6 = (bf16[288,1280]{1,0:T(8,128)(2,1)S(1)}, bf16[288,1280]{1,0:T(8,128)(2,1)S(1)}, u32[]{:S(2)}, u32[]{:S(2)}) collective-permute-start(bf16[288,1280]{1,0:T(8,128)(2,1)S(1)} %pad_maximum_fusion.2.refs_0_), channel_id=1, source_target_pairs={{0,96},{1,97},{16,112},{17,113},{2,98},{3,99},{18,114},{19,115},{4... | collective-permute-start | bytes 2211848 | tf_op jit(solution)/shard_map/ppermute | solution.py:56
  53.8 34.1 %collective-permute-start.7 = (bf16[288,1280]{1,0:T(8,128)(2,1)S(1)}, bf16[288,1280]{1,0:T(8,128)(2,1)S(1)}, u32[]{:S(2)}, u32[]{:S(2)}) collective-permute-start(bf16[288,1280]{1,0:T(8,128)(2,1)S(1)} %pad_maximum_fusion.2.refs_0_), channel_id=1, source_target_pairs={{0,64},{1,65},{16,80},{17,81},{2,66},{3,67},{18,82},{19,83},{4,68}... | collective-permute-start | bytes 2211848 | tf_op jit(solution)/shard_map/ppermute | solution.py:56
  56.5 49.8 %collective-permute-start.3 = (bf16[704,1152]{1,0:T(8,128)(2,1)}, bf16[704,1152]{1,0:T(8,128)(2,1)}, u32[]{:S(2)}, u32[]{:S(2)}) collective-permute-start(bf16[704,1152]{1,0:T(8,128)(2,1)} %pad_maximum_fusion), channel_id=1, source_target_pairs={{0,1},{1,0},{16,17},{17,16},{2,3},{3,2},{18,19},{19,18},{4,5},{5,4... | collective-permute-start | bytes 4866056 | tf_op jit(solution)/shard_map/ppermute | solution.py:56
  92.8 30.8 %collective-permute-start.15 = (bf16[1152,1280]{1,0:T(8,128)(2,1)}, bf16[1152,1280]{1,0:T(8,128)(2,1)}, u32[]{:S(2)}, u32[]{:S(2)}) collective-permute-start(bf16[1152,1280]{1,0:T(8,128)(2,1)} %get-tuple-element.32.refs_7_.refs_4_), channel_id=1, source_target_pairs={{0,1},{1,0},{16,17},{17,16},{2,3},{3,2},{18,19},{19,18},{4,5},{5,4... | collective-permute-start | bytes 8847368 | tf_op jit(solution)/shard_map/ppermute | solution.py:56
  105.5 18.2 %collective-permute-start.14 = (bf16[640,1280]{1,0:T(8,128)(2,1)S(1)}, bf16[640,1280]{1,0:T(8,128)(2,1)S(1)}, u32[]{:S(2)}, u32[]{:S(2)}) collective-permute-start(bf16[640,1280]{1,0:T(8,128)(2,1)S(1)} %get-tuple-element.39), channel_id=1, source_target_pairs={{0,1},{1,0},{16,17},{17,16},{2,3},{3,2},{18,19},{19,18},{4,5},{5,4... | collective-permute-start | bytes 4915208 | tf_op jit(solution)/shard_map/ppermute | solution.py:56
  113.4 10.3 %collective-permute-start.8 = (bf16[640,1280]{1,0:T(8,128)(2,1)S(1)}, bf16[640,1280]{1,0:T(8,128)(2,1)S(1)}, u32[]{:S(2)}, u32[]{:S(2)}) collective-permute-start(bf16[640,1280]{1,0:T(8,128)(2,1)S(1)} %get-tuple-element.34), channel_id=1, source_target_pairs={{0,1},{1,0},{16,17},{17,16},{2,3},{3,2},{18,19},{19,18},{4,5},{5,4... | collective-permute-start | bytes 4915208 | tf_op jit(solution)/shard_map/ppermute | solution.py:56
  136.2 21.0 %collective-permute-start.18 = (bf16[320,1152]{1,0:T(8,128)(2,1)S(1)}, bf16[320,1152]{1,0:T(8,128)(2,1)}, u32[]{:S(2)}, u32[]{:S(2)}) collective-permute-start(bf16[320,1152]{1,0:T(8,128)(2,1)S(1)} %get-tuple-element.51), channel_id=1, source_target_pairs={{0,8},{1,9},{16,24},{17,25},{2,10},{3,11},{18,26},{19,27},{4,12},{... | collective-permute-start | bytes 2211848 | tf_op jit(solution)/shard_map/ppermute | solution.py:56
  137.6 34.7 %collective-permute-start.17 = (bf16[320,1152]{1,0:T(8,128)(2,1)}, bf16[320,1152]{1,0:T(8,128)(2,1)}, u32[]{:S(2)}, u32[]{:S(2)}) collective-permute-start(bf16[320,1152]{1,0:T(8,128)(2,1)} %get-tuple-element.50), channel_id=1, source_target_pairs={{0,4},{1,5},{16,20},{17,21},{2,6},{3,7},{18,22},{19,23},{4,8},{5,9... | collective-permute-start | bytes 2211848 | tf_op jit(solution)/shard_map/ppermute | solution.py:56
  139.9 32.7 %collective-permute-start.16 = (bf16[320,1152]{1,0:T(8,128)(2,1)}, bf16[320,1152]{1,0:T(8,128)(2,1)}, u32[]{:S(2)}, u32[]{:S(2)}) collective-permute-start(bf16[320,1152]{1,0:T(8,128)(2,1)} %get-tuple-element.49), channel_id=1, source_target_pairs={{0,12},{1,13},{16,28},{17,29},{2,14},{3,15},{18,30},{19,31},{4,0},... | collective-permute-start | bytes 2211848 | tf_op jit(solution)/shard_map/ppermute | solution.py:56
  140.8 34.4 %collective-permute-start.22 = (bf16[304,1280]{1,0:T(8,128)(2,1)}, bf16[304,1280]{1,0:T(8,128)(2,1)}, u32[]{:S(2)}, u32[]{:S(2)}) collective-permute-start(bf16[304,1280]{1,0:T(8,128)(2,1)} %get-tuple-element.56), channel_id=1, source_target_pairs={{0,64},{1,65},{16,80},{17,81},{2,66},{3,67},{18,82},{19,83},{4,68}... | collective-permute-start | bytes 2334728 | tf_op jit(solution)/shard_map/ppermute | solution.py:56
  142.6 34.1 %collective-permute-start.21 = (bf16[304,1280]{1,0:T(8,128)(2,1)}, bf16[304,1280]{1,0:T(8,128)(2,1)}, u32[]{:S(2)}, u32[]{:S(2)}) collective-permute-start(bf16[304,1280]{1,0:T(8,128)(2,1)} %get-tuple-element.55), channel_id=1, source_target_pairs={{0,32},{1,33},{16,48},{17,49},{2,34},{3,35},{18,50},{19,51},{4,36}... | collective-permute-start | bytes 2334728 | tf_op jit(solution)/shard_map/ppermute | solution.py:56
  157.1 21.1 %collective-permute-start.20 = (bf16[304,1280]{1,0:T(8,128)(2,1)}, bf16[304,1280]{1,0:T(8,128)(2,1)}, u32[]{:S(2)}, u32[]{:S(2)}) collective-permute-start(bf16[304,1280]{1,0:T(8,128)(2,1)} %get-tuple-element.54), channel_id=1, source_target_pairs={{0,96},{1,97},{16,112},{17,113},{2,98},{3,99},{18,114},{19,115},{4... | collective-permute-start | bytes 2334728 | tf_op jit(solution)/shard_map/ppermute | solution.py:56
  174.5 13.1 %collective-permute-start.19 = (bf16[160,1152]{1,0:T(8,128)(2,1)S(1)}, bf16[160,1152]{1,0:T(8,128)(2,1)S(1)}, u32[]{:S(2)}, u32[]{:S(2)}) collective-permute-start(bf16[160,1152]{1,0:T(8,128)(2,1)S(1)} %slice.38), channel_id=1, source_target_pairs={{0,2},{1,3},{16,18},{17,19},{2,0},{3,1},{18,16},{19,17},{4,6},{5,7... | collective-permute-start | bytes 1105928 | tf_op jit(solution)/shard_map/ppermute | solution.py:56
  180.3 12.9 %collective-permute-start.23 = (bf16[160,1280]{1,0:T(8,128)(2,1)S(1)}, bf16[160,1280]{1,0:T(8,128)(2,1)S(1)}, u32[]{:S(2)}, u32[]{:S(2)}) collective-permute-start(bf16[160,1280]{1,0:T(8,128)(2,1)S(1)} %pad_maximum_fusion.3), channel_id=1, source_target_pairs={{0,16},{1,17},{16,0},{17,1},{2,18},{3,19},{18,2},{19,3},{4,20},{5,... | collective-permute-start | bytes 1228808 | tf_op jit(solution)/shard_map/ppermute | solution.py:56
  (13 other events, 55.5 us)

commit v2 on v1

--- a/solution.py
+++ b/solution.py
@@ -127,7 +127,7 @@
         in_specs=[SMEM] + [VMEM] * len(pieces),
         out_specs=[VMEM] * 3,
         compiler_params=params(12),
-        cost_estimate=cost(0, 32 * depth * width),
+        cost_estimate=cost(10_000_000_000, 32 * depth * width),
         name="text_units",
     )(place, *pieces)
 
@@ -135,32 +135,36 @@
 def weight_kernel(rows, scalars, first_text, *refs):
     pieces, text, (image, weight, other) = refs[:-4], refs[-4], refs[-3:]
     half = rows // 2
+    halves = []
+    for piece in pieces:
+        done = 0
+        while done < piece.shape[0]:
+            halves.append((piece, done))
+            done += half + TAIL if len(halves) % 2 else half
     slope, shift = scalars[0], scalars[1]
     columns = text.shape[1]
     eye = lax.broadcasted_iota(jnp.int32, (rows, rows), 0) == lax.broadcasted_iota(
         jnp.int32, (rows, rows), 1
     )
     names = (lax.broadcasted_iota(jnp.int32, (rows, columns), 1) + first_text[0]).astype(F32)
-    block = 0
-    for piece in pieces:
-        for start in range(0, piece.shape[0], rows + TAIL):
-            at = block * rows
-            image[at : at + half, :] = piece[start : start + half, :]
-            image[at + half : at + rows, :] = piece[start + half + TAIL : start + rows + TAIL, :]
-            tail = piece[start + half : start + half + TAIL, :rows].astype(F32)
-            product = lax.dot_general(
-                image[at : at + rows, :], text[...], NN, preferred_element_type=F32
-            )
-            chance = 1.0 / (1.0 + jnp.exp2(product * slope + shift))
-            match = jnp.sum(
-                jnp.where(eye, tail[0:1] * 256.0 + tail[1:2], 0.0), axis=1, keepdims=True
-            )
-            value = (chance - jnp.where(match == names, 1.0, 0.0)).astype(BF16)
-            weight[at : at + rows, :] = value
-            if block >= 4:
-                at -= 4 * rows
-                other[at : at + rows, :] = value
-            block += 1
+    for block in range(8):
+        (a, i), (b, j) = halves[2 * block : 2 * block + 2]
+        at = block * rows
+        image[at : at + half, :] = a[i : i + half, :]
+        image[at + half : at + rows, :] = b[j : j + half, :]
+        tail = a[i + half : i + half + TAIL, :rows].astype(F32)
+        product = lax.dot_general(
+            image[at : at + rows, :], text[...], NN, preferred_element_type=F32
+        )
+        chance = 1.0 / (1.0 + jnp.exp2(product * slope + shift))
+        match = jnp.sum(
+            jnp.where(eye, tail[0:1] * 256.0 + tail[1:2], 0.0), axis=1, keepdims=True
+        )
+        value = (chance - jnp.where(match == names, 1.0, 0.0)).astype(BF16)
+        weight[at : at + rows, :] = value
+        if block >= 4:
+            at -= 4 * rows
+            other[at : at + rows, :] = value
 
 
 def weights(scalars, first_text, pieces, rows, text):
@@ -182,7 +186,7 @@
 
 
 def text_back_kernel(place, image_a, weight_a, image_b, weight_b, raw, *refs):
-    outs, back = refs[:4], refs[4]
+    outs, back = refs[:5], refs[5]
     width, columns = back.shape
     block = 384
     dots = jnp.zeros((1, columns), F32)
@@ -199,10 +203,16 @@
     depth = width // 4
     for i in range(4):
         start = pl.multiple_of(place[2 * i] // 2 * depth, 8)
-        out = outs[i]
-        out[:depth, :] = back[pl.ds(start, depth), :].astype(out.dtype)
         spread = [empty] * 3 * i + list(tail) + [empty] * (TAIL - 3 * i - 3)
-        out[depth:, :] = jnp.concatenate(spread, 0).astype(out.dtype)
+        spread = jnp.concatenate(spread, 0)
+        if i < 3:
+            outs[i][:depth, :] = back[pl.ds(start, depth), :].astype(outs[i].dtype)
+            outs[i][depth:, :] = spread.astype(outs[i].dtype)
+        else:
+            half = depth // 2
+            outs[3][...] = back[pl.ds(start, half), :].astype(BF16)
+            outs[4][:half, :] = back[pl.ds(start + half, half), :].astype(BF16)
+            outs[4][half:, :] = spread.astype(BF16)
 
 
 def text_terms(place, image_a, weight_a, image_b, weight_b, raw):
@@ -211,9 +221,15 @@
     shape = (width // 4 + TAIL, columns)
     return pl.pallas_call(
         text_back_kernel,
-        out_shape=[jax.ShapeDtypeStruct(shape, F32)] + [jax.ShapeDtypeStruct(shape, BF16)] * 3,
+        out_shape=[
+            jax.ShapeDtypeStruct(shape, F32),
+            jax.ShapeDtypeStruct(shape, BF16),
+            jax.ShapeDtypeStruct(shape, BF16),
+            jax.ShapeDtypeStruct((width // 8, columns), BF16),
+            jax.ShapeDtypeStruct((width // 8 + TAIL, columns), BF16),
+        ],
         in_specs=[SMEM] + [VMEM] * 5,
-        out_specs=[VMEM] * 4,
+        out_specs=[VMEM] * 5,
         scratch_shapes=[pltpu.VMEM((width, columns), F32)],
         compiler_params=params(16),
         cost_estimate=cost(4 * count * width * columns, 4 * count * columns),
@@ -222,59 +238,116 @@
 
 
 def image_back_kernel(rows, own_a, got_a, own_b, got_b, text, text_got, *outs):
-    for h, (own, got) in enumerate(((own_a, got_a), (own_b, got_b))):
-        back = lax.dot_general(
-            own[: 4 * rows, :], text[...], NT, preferred_element_type=F32
-        ) + lax.dot_general(got[...], text_got[...], NT, preferred_element_type=F32)
-        for k in range(4):
-            out = outs[k]
-            out[h * rows : (h + 1) * rows, :] = back[k * rows : (k + 1) * rows].astype(out.dtype)
+    for start in (2, 0):
+        block = slice(start * rows, (start + 2) * rows)
+        for h, (own, got) in enumerate(((own_a, got_a), (own_b, got_b))):
+            back = lax.dot_general(
+                own[block, :], text[...], NT, preferred_element_type=F32
+            ) + lax.dot_general(got[block, :], text_got[...], NT, preferred_element_type=F32)
+            for k in range(2):
+                i = start + k
+                mine = back[k * rows : (k + 1) * rows]
+                if i == 3:
+                    outs[3 + h][...] = mine.astype(BF16)
+                else:
+                    outs[i][h * rows : (h + 1) * rows, :] = mine.astype(outs[i].dtype)
 
 
 def image_terms(rows, own_a, got_a, own_b, got_b, text, text_got):
     width, columns = text.shape
-    kinds = [F32, BF16, BF16, BF16]
+    kinds = [(2 * rows, F32), (2 * rows, BF16), (2 * rows, BF16), (rows, BF16), (rows, BF16)]
     return pl.pallas_call(
         lambda *refs: image_back_kernel(rows, *refs),
-        out_shape=[jax.ShapeDtypeStruct((2 * rows, width), kind) for kind in kinds],
+        out_shape=[jax.ShapeDtypeStruct((count, width), kind) for count, kind in kinds],
         in_specs=[VMEM] * 6,
-        out_specs=[VMEM] * 4,
+        out_specs=[VMEM] * 5,
         compiler_params=params(16),
-        cost_estimate=cost(32 * rows * width * columns, 8 * width * columns),
+        cost_estimate=cost(10_000_000_000, 8 * width * columns),
         name="image_terms",
     )(own_a, got_a, own_b, got_b, text, text_got)
 
 
-def ring_sum(parts, axis):
-    far = [send(part, (axis, s)) for s, part in zip(STEPS[1:], parts[1:])]
-    return parts[0] + sum(part.astype(F32) for part in far)
-
-
-def text_final_kernel(temper, low, total, given, raw, inverse, out):
+def add_kernel(at, value, more, out):
+    rows = more.shape[0]
+    for start in range(0, value.shape[0], 16):
+        block = slice(start, start + 16)
+        if at <= start < at + rows:
+            total = value[block, :].astype(F32) + more[start - at : start - at + 16, :].astype(F32)
+            out[block, :] = total.astype(BF16)
+        else:
+            out[block, :] = value[block, :]
+
+
+def add_rows(value, more, at):
+    return pl.pallas_call(
+        lambda *refs: add_kernel(at, *refs),
+        out_shape=jax.ShapeDtypeStruct(value.shape, BF16),
+        in_specs=[VMEM] * 2,
+        out_specs=VMEM,
+        compiler_params=params(8),
+        cost_estimate=cost(0, 6 * value.size),
+        name="add_rows",
+    )(value, more)
+
+
+def ring_terms(parts, far, axis):
+    far = [send(far[0], (axis, 1)), send(far[1], (axis, -1))]
+    ahead = add_rows(parts[2], far[0], 0)
+    back = add_rows(parts[1], far[1], far[0].shape[0])
+    return parts[0], send(ahead, (axis, 1)), send(back, (axis, -1))
+
+
+def halves_kernel(which, own, ahead, back, keep, give):
+    size = keep.shape[0]
+    rest = own.shape[0] - 2 * size
+    mine = pl.multiple_of(which[0] * size, 16)
+    other = pl.multiple_of((1 - which[0]) * size, 16)
+
+    def total(rows):
+        return own[rows, :] + ahead[rows, :].astype(F32) + back[rows, :].astype(F32)
+
+    keep[...] = total(pl.ds(mine, size))
+    give[:size, :] = total(pl.ds(other, size)).astype(BF16)
+    if rest:
+        give[size:, :] = total(pl.ds(2 * size, rest)).astype(BF16)
+
+
+def sum_halves(which, own, ahead, back, size):
+    rows, width = own.shape
+    return pl.pallas_call(
+        halves_kernel,
+        out_shape=[
+            jax.ShapeDtypeStruct((size, width), F32),
+            jax.ShapeDtypeStruct((rows - size, width), BF16),
+        ],
+        in_specs=[SMEM] + [VMEM] * 3,
+        out_specs=[VMEM] * 2,
+        compiler_params=params(8),
+        cost_estimate=cost(0, 12 * own.size),
+        name="sum_halves",
+    )(which, own, ahead, back)
+
+
+def text_final_kernel(temper, keep, gave, given, raw, inverse, out):
     depth = raw.shape[0]
     scale = inverse[...]
-    keep = total[pl.ds(pl.multiple_of(low[0] * depth, 8), depth), :]
-    back = keep + given[:depth, :].astype(F32)
-    tails = total[2 * depth :, :] + given[depth:, :].astype(F32)
+    back = keep[...] + given[:depth, :].astype(F32)
+    tails = gave[depth:, :].astype(F32) + given[depth:, :].astype(F32)
     dots = jnp.sum(tails, axis=0, keepdims=True) * scale
     unit = raw[...].astype(F32) * scale
     out[...] = (temper[0] * (back - unit * dots) * scale).astype(BF16)
 
 
-def text_final(temper, low, total, given, raw, inverse):
+def text_final(temper, keep, gave, given, raw, inverse):
     return pl.pallas_call(
         text_final_kernel,
         out_shape=jax.ShapeDtypeStruct(raw.shape, BF16),
-        in_specs=[SMEM, SMEM] + [VMEM] * 4,
+        in_specs=[SMEM] + [VMEM] * 5,
         out_specs=VMEM,
         compiler_params=params(8),
-        cost_estimate=cost(0, 4 * raw.size),
+        cost_estimate=cost(0, 12 * raw.size),
         name="text_final",
-    )(temper, low, total, given, raw, inverse)
-
-
-def gather_ring(piece, axis):
-    return [piece] + [send(piece, (axis, -s if s < 2 else s)) for s in STEPS[1:]]
+    )(temper, keep, gave, given, raw, inverse)
 
 
 def local(image, text, pair_text, log_scale, bias):
@@ -289,37 +362,51 @@
     own_text = text.T
     text_lo = send(own_text, "lo")
     unit, image_inverse = image_units(image, pair_text)
-    near = [unit, send(unit, ("y", 1)), send(unit, ("y", -1))]
-    near.append(send(after(unit, *near[1:]), ("y", 2)))
-    text_pieces = gather_ring(jnp.concatenate([own_text, text_lo], 0), "x")
+    a, b = send(unit, ("y", 1)), send(unit, ("y", -1))
+    text2 = jnp.concatenate([own_text, text_lo], 0)
+    text_a, text_b = send(text2, ("x", 1)), send(text2, ("x", -1))
     unit_hi = send(after(unit, text_lo), "hi")
-    unit_hi = after(unit_hi, near[3])
-    partner = [unit_hi, send(unit_hi, ("y", 1)), send(unit_hi, ("y", -1))]
-    partner.append(send(after(unit_hi, *partner[1:]), ("y", 2)))
-    near.append(send(jnp.concatenate(near, 0), "core"))
-    partner.append(send(jnp.concatenate(partner, 0), "core"))
+    cut = rows // 2 + TAIL
+    a2, b2 = send(a[:cut], ("y", 1)), send(b[cut:], ("y", -1))
+    unit_hi = after(unit_hi, a2, b2)
+    c, d = send(unit_hi, ("y", 1)), send(unit_hi, ("y", -1))
+    text_a2, text_b2 = send(text_a[:depth], ("x", 1)), send(text_b[depth:], ("x", -1))
+    c, d, text_a, text_b = lax.optimization_barrier((c, d, text_a, text_b))
+    c2, d2 = send(c[:cut], ("y", 1)), send(d[cut:], ("y", -1))
+    near, partner = [unit, a, b, a2, b2], [unit_hi, c, d, c2, d2]
+    near.append(after(send(jnp.concatenate(near, 0), "core"), c2, d2))
+    partner += [
+        send(jnp.concatenate(partner[:3], 0), "core"),
+        send(jnp.concatenate(partner[3:], 0), "core"),
+    ]
+    text_pieces = [text2, text_a, text_b, text_a2, text_b2]
 
     text_unit, text_raw, text_inverse = text_units(place, text_pieces, depth)
-    text_got = send(text_unit, "core")
     image_a, weight_a, other_a = weights(scalars, first_text, near, rows, text_unit)
     got_a = send(other_a, "core")
-    image_b, weight_b, other_b = weights(scalars, first_text, partner, rows, text_unit)
+    text_got = send(after(text_unit, other_a), "core")
+    image_b, weight_b, other_b = weights(
+        after(scalars, other_a), first_text, partner, rows, text_unit
+    )
     got_b = send(other_b, "core")
-    text_parts = text_terms(place, image_a, weight_a, image_b, weight_b, text_raw)
-    got_b, *text_parts = lax.optimization_barrier((got_b, *text_parts))
-    image_parts = image_terms(rows, weight_a, got_a, weight_b, got_b, text_unit, text_got)
-
-    image_back = ring_sum(image_parts, "y")
-    image_back = image_back[:rows] + send(image_back[rows:].astype(BF16), "hi").astype(F32)
+    *text_parts, far0, far1 = text_terms(place, image_a, weight_a, image_b, weight_b, text_raw)
+    got_b, far0, far1, *text_parts = lax.optimization_barrier((got_b, far0, far1, *text_parts))
+    *image_parts, image_far0, image_far1 = image_terms(
+        rows, weight_a, got_a, weight_b, got_b, text_unit, text_got
+    )
+
+    *text_parts, _ = lax.optimization_barrier((*text_parts, image_parts[1]))
+    text_terms_here = ring_terms(text_parts, (far0, far1), "x")
+    image_terms_here = ring_terms(image_parts, (image_far0, image_far1), "y")
+    keep, gave = sum_halves(lo[None], *text_terms_here, depth)
+    given = send(gave, "lo")
+    grad_text = text_final(temper[None], keep, gave, given, own_text, text_inverse).T
+
+    keep, gave = sum_halves(jnp.zeros((1,), jnp.int32), *image_terms_here, rows)
+    image_back = keep + send(gave, "hi").astype(F32)
     image_dir = image.astype(F32) * image_inverse
     dot = jnp.sum(image_dir * image_back, axis=-1, keepdims=True)
     grad_image = temper * (image_back - image_dir * dot) * image_inverse
-
-    total = ring_sum(text_parts, "x")
-    low_half, high_half, tail = total[:depth], total[depth : 2 * depth], total[2 * depth :]
-    give = jnp.where(lo == 0, high_half, low_half)
-    given = send(jnp.concatenate([give, tail], 0).astype(BF16), "lo")
-    grad_text = text_final(temper[None], lo[None], total, given, own_text, text_inverse).T
     return grad_image.astype(BF16), grad_text
 
 

time: 195 us -> 138 us (0.71)
  waiting for transfers between devices: 107 us -> 47.7 us
  starting transfers between devices: 28.5 us -> 40.3 us
  Pallas kernels: 41.3 us -> 34 us
  other arithmetic: 8.06 us -> 4.64 us
    ppermute x24 -> x30, waiting for transfers between devices: 107 us -> 47.7 us  [send(): return lax.ppermute(value, AXES, MOVES[move])]
    ppermute x24 -> x30, starting transfers between devices: 28.5 us -> 40.3 us  [send(): return lax.ppermute(value, AXES, MOVES[move])]
    pallas_call x1, Pallas kernels: 12.5 us -> 8.64 us  [image_terms(): pl.pallas_call(lambda *refs: image_back_kernel(rows, *refs), out_shape=[j...]
    add x2 -> x0, other arithmetic: 3.81 us -> none  [ring_sum(): return parts[0] + sum((part.astype(F32) for part in far))]
    pallas_call x2, Pallas kernels: 14.3 us -> 11.4 us  [weights(): pl.pallas_call(lambda *refs: weight_kernel(rows, *refs), out_shape=[jax.S...]
    slice x2 -> x6, local copies, waits for them, and re-layouts: 0.05 us -> 2.09 us  [the longest x1 1.02 us: local(): text_a[:depth]]
    unnamed x42 -> x14, local copies, waits for them, and re-layouts: 6.69 us -> 4.75 us
  transfers between devices with their start and end apart: 24 -> 30, of which waited for: 14 -> 11; matrix products, arithmetic and copies ran while one was open for 4% -> 6% of each run, Pallas kernels for 14% -> 25%
where the time goes in v2:
time: 138 us; the launch traced here: 137 us
  waiting for transfers between devices  47.7 us (35%)
  starting transfers between devices  40.3 us (29%)
  Pallas kernels  34 us (25%)
  local copies, waits for them, and re-layouts  8.31 us (6%)
  other arithmetic  4.64 us (3%)
  between operations  2.2 us (2%)
    ppermute x30, waiting for transfers between devices, send(): return lax.ppermute(value, AXES, MOVES[move])  47.7 us
    ppermute x30, starting transfers between devices, send(): return lax.ppermute(value, AXES, MOVES[move])  40.3 us
    pallas_call x2, Pallas kernels, weights(): pl.pallas_call(lambda *refs: weight_kernel(rows, *refs), out_shape=[jax.S...  11.4 us
    pallas_call x1, Pallas kernels, text_terms(): pl.pallas_call(text_back_kernel, out_shape=[jax.ShapeDtypeStruct(shape, F...  8.73 us
    pallas_call x1, Pallas kernels, image_terms(): pl.pallas_call(lambda *refs: image_back_kernel(rows, *refs), out_shape=[j...  8.64 us
    unnamed x14, local copies, waits for them, and re-layouts  4.75 us
  transfers between devices with their start and end apart: 30, of which 11 were waited for; matrix products, arithmetic and copies ran while one was open for 6% of the time, Pallas kernels for 25%

profile of v2, /device:TPU:6, one launch (start us, length us, event | category | flops | bytes accessed | tf_op | source)
XLA Modules:
  0.0 137.2 jit_solution(10306526467214211604)
XLA Ops:
  0.6 2.0 %collective-permute-start.5 = (bf16[144,1280]{1,0:T(8,128)(2,1)}, bf16[144,1280]{1,0:T(8,128)(2,1)S(1)}, u32[]{:S(2)}, u32[]{:S(2)}) collective-permute-start(bf16[144,1280]{1,0:T(8,128)(2,1)} %bitcast.15), channel_id=1, source_target_pairs={{0,16},{1,17},{16,0},{17,1},{2,18},{3,19},{18,2},{19,3},{4,20},{5,... | collective-permute-start | bytes 1105928 | tf_op jit(solution)/shard_map/ppermute | solution.py:56
  4.5 1.6 %collective-permute-start = (bf16[176,1152]{1,0:T(8,128)(2,1)S(1)}, bf16[176,1152]{1,0:T(8,128)(2,1)S(1)}, u32[]{:S(2)}, u32[]{:S(2)}) collective-permute-start(bf16[176,1152]{1,0:T(8,128)(2,1)S(1)} %get-tuple-element.46.refs_2_), channel_id=1, source_target_pairs={{0,4},{1,5},{16,20},{17,21},{2,6},{3,7},{18,22},{19,23},{4,8},{5,9... | collective-permute-start | bytes 1216520 | tf_op jit(solution)/shard_map/ppermute | solution.py:56
  6.1 1.7 %collective-permute-start.1 = (bf16[176,1152]{1,0:T(8,128)(2,1)S(1)}, bf16[176,1152]{1,0:T(8,128)(2,1)S(1)}, u32[]{:S(2)}, u32[]{:S(2)}) collective-permute-start(bf16[176,1152]{1,0:T(8,128)(2,1)S(1)} %get-tuple-element.46.refs_2_), channel_id=1, source_target_pairs={{0,12},{1,13},{16,28},{17,29},{2,14},{3,15},{18,30},{19,31},{4,0},... | collective-permute-start | bytes 1216520 | tf_op jit(solution)/shard_map/ppermute | solution.py:56
  8.6 2.9 %collective-permute-done.5 = bf16[144,1280]{1,0:T(8,128)(2,1)S(1)} collective-permute-done((bf16[144,1280]{1,0:T(8,128)(2,1)}, bf16[144,1280]{1,0:T(8,128)(2,1)S(1)}, u32[]{:S(2)}, u32[]{:S(2)}) %collective-permute-start.5) | collective-permute-done | bytes 368672 | tf_op jit(solution)/shard_map/ppermute | solution.py:56
  13.0 1.5 %collective-permute-start.10 = (bf16[288,1280]{1,0:T(8,128)(2,1)S(1)}, bf16[288,1280]{1,0:T(8,128)(2,1)}, u32[]{:S(2)}, u32[]{:S(2)}) collective-permute-start(bf16[288,1280]{1,0:T(8,128)(2,1)S(1)} %pad_maximum_fusion.1.refs_0_), channel_id=1, source_target_pairs={{0,96},{1,97},{16,112},{17,113},{2,98},{3,99},{18,114},{19,115},{4... | collective-permute-start | bytes 2211848 | tf_op jit(solution)/shard_map/ppermute | solution.py:56
  14.6 3.7 %collective-permute-start.6 = (bf16[176,1152]{1,0:T(8,128)(2,1)S(1)}, bf16[176,1152]{1,0:T(8,128)(2,1)S(1)}, u32[]{:S(2)}, u32[]{:S(2)}) collective-permute-start(bf16[176,1152]{1,0:T(8,128)(2,1)S(1)} %get-tuple-element.46.refs_2_), channel_id=1, source_target_pairs={{0,2},{1,3},{16,18},{17,19},{2,0},{3,1},{18,16},{19,17},{4,6},{5,7... | collective-permute-start | bytes 1216520 | tf_op jit(solution)/shard_map/ppermute | solution.py:56
  18.3 1.6 %collective-permute-start.2 = (bf16[96,1152]{1,0:T(8,128)(2,1)S(1)}, bf16[96,1152]{1,0:T(8,128)(2,1)S(1)}, u32[]{:S(2)}, u32[]{:S(2)}) collective-permute-start(bf16[96,1152]{1,0:T(8,128)(2,1)S(1)} %slice.24), channel_id=1, source_target_pairs={{0,4},{1,5},{16,20},{17,21},{2,6},{3,7},{18,22},{19,23},{4,8},{5,9... | collective-permute-start | bytes 663560 | tf_op jit(solution)/shard_map/ppermute | solution.py:56
  20.0 1.7 %collective-permute-start.3 = (bf16[80,1152]{1,0:T(8,128)(2,1)S(1)}, bf16[80,1152]{1,0:T(8,128)(2,1)S(1)}, u32[]{:S(2)}, u32[]{:S(2)}) collective-permute-start(bf16[80,1152]{1,0:T(8,128)(2,1)S(1)} %slice.25), channel_id=1, source_target_pairs={{0,12},{1,13},{16,28},{17,29},{2,14},{3,15},{18,30},{19,31},{4,0},... | collective-permute-start | bytes 552968 | tf_op jit(solution)/shard_map/ppermute | solution.py:56
  23.3 2.2 %collective-permute-done.2.refs_5_ = bf16[96,1152]{1,0:T(8,128)(2,1)S(1)} collective-permute-done((bf16[96,1152]{1,0:T(8,128)(2,1)S(1)}, bf16[96,1152]{1,0:T(8,128)(2,1)S(1)}, u32[]{:S(2)}, u32[]{:S(2)}) %collective-permute-start.2) | collective-permute-done | bytes 221216 | tf_op jit(solution)/shard_map/ppermute | solution.py:56
  26.2 1.6 %collective-permute-start.7 = (bf16[176,1152]{1,0:T(8,128)(2,1)S(1)}, bf16[176,1152]{1,0:T(8,128)(2,1)S(1)}, u32[]{:S(2)}, u32[]{:S(2)}) collective-permute-start(bf16[176,1152]{1,0:T(8,128)(2,1)S(1)} %collective-permute-done.6.refs_2_), channel_id=1, source_target_pairs={{0,4},{1,5},{16,20},{17,21},{2,6},{3,7},{18,22},{19,23},{4,8},{5,9... | collective-permute-start | bytes 1216520 | tf_op jit(solution)/shard_map/ppermute | solution.py:56
  27.8 1.7 %collective-permute-start.8 = (bf16[176,1152]{1,0:T(8,128)(2,1)S(1)}, bf16[176,1152]{1,0:T(8,128)(2,1)S(1)}, u32[]{:S(2)}, u32[]{:S(2)}) collective-permute-start(bf16[176,1152]{1,0:T(8,128)(2,1)S(1)} %collective-permute-done.6.refs_2_), channel_id=1, source_target_pairs={{0,12},{1,13},{16,28},{17,29},{2,14},{3,15},{18,30},{19,31},{4,0},... | collective-permute-start | bytes 1216520 | tf_op jit(solution)/shard_map/ppermute | solution.py:56
  33.3 1.8 %collective-permute-start.13 = (bf16[144,1280]{1,0:T(8,128)(2,1)S(1)}, bf16[144,1280]{1,0:T(8,128)(2,1)S(1)}, u32[]{:S(2)}, u32[]{:S(2)}) collective-permute-start(bf16[144,1280]{1,0:T(8,128)(2,1)S(1)} %slice.26), channel_id=1, source_target_pairs={{0,32},{1,33},{16,48},{17,49},{2,34},{3,35},{18,50},{19,51},{4,36}... | collective-permute-start | bytes 1105928 | tf_op jit(solution)/shard_map/ppermute | solution.py:56
  36.6 1.6 %collective-permute-start.11 = (bf16[96,1152]{1,0:T(8,128)(2,1)S(1)}, bf16[96,1152]{1,0:T(8,128)(2,1)S(1)}, u32[]{:S(2)}, u32[]{:S(2)}) collective-permute-start(bf16[96,1152]{1,0:T(8,128)(2,1)S(1)} %slice.20), channel_id=1, source_target_pairs={{0,4},{1,5},{16,20},{17,21},{2,6},{3,7},{18,22},{19,23},{4,8},{5,9... | collective-permute-start | bytes 663560 | tf_op jit(solution)/shard_map/ppermute | solution.py:56
  38.2 1.7 %collective-permute-start.12 = (bf16[80,1152]{1,0:T(8,128)(2,1)S(1)}, bf16[80,1152]{1,0:T(8,128)(2,1)S(1)}, u32[]{:S(2)}, u32[]{:S(2)}) collective-permute-start(bf16[80,1152]{1,0:T(8,128)(2,1)S(1)} %slice.21), channel_id=1, source_target_pairs={{0,12},{1,13},{16,28},{17,29},{2,14},{3,15},{18,30},{19,31},{4,0},... | collective-permute-start | bytes 552968 | tf_op jit(solution)/shard_map/ppermute | solution.py:56
  40.1 4.3 %collective-permute-done.13.refs_3_ = bf16[144,1280]{1,0:T(8,128)(2,1)S(1)} collective-permute-done((bf16[144,1280]{1,0:T(8,128)(2,1)S(1)}, bf16[144,1280]{1,0:T(8,128)(2,1)S(1)}, u32[]{:S(2)}, u32[]{:S(2)}) %collective-permute-start.13) | collective-permute-done | bytes 368672 | tf_op jit(solution)/shard_map/ppermute | solution.py:56
  44.4 3.7 %collective-permute-done.14.refs_4_ = bf16[144,1280]{1,0:T(8,128)(2,1)S(1)} collective-permute-done((bf16[144,1280]{1,0:T(8,128)(2,1)S(1)}, bf16[144,1280]{1,0:T(8,128)(2,1)S(1)}, u32[]{:S(2)}, u32[]{:S(2)}) %collective-permute-start.14) | collective-permute-done | bytes 368672 | tf_op jit(solution)/shard_map/ppermute | solution.py:56
  48.1 2.5 %text_units.1 = (bf16[1152,1280]{1,0:T(8,128)(2,1)S(1)}, bf16[1152,1280]{1,0:T(8,128)(2,1)S(1)}, f32[1,1280]{1,0:T(1,128)S(1)}) custom-call(s32[8]{0:T(128)S(1)} %stack.44.place, bf16[288,1280]{1,0:T(8,128)(2,1)S(1)} %pad_maximum_fusion.1.refs_0_, bf16[288,1280]{1,0:T(8,128)(2,1)} %collective-permute-done.9.refs_1_, ...), custom_call_target="tpu_custom_call" | custom-call | flops 10000000000 | bytes 5898240 | tf_op jit(solution)/shard_map/text_units/pallas_call | solution.py:124
  50.6 6.2 %weights.2 = (bf16[1280,1152]{1,0:T(8,128)(2,1)S(1)}, bf16[1280,1280]{1,0:T(8,128)(2,1)S(1)}, bf16[640,1280]{1,0:T(8,128)(2,1)S(1)}) custom-call(f32[2]{0:T(128)S(1)} %pad_maximum_fusion.3.refs_0_, s32[1]{0:T(128)} %bitcast.2.refs_1_, bf16[176,1152]{1,0:T(8,128)(2,1)S(1)} %get-tuple-element.46.refs_2_, bf16[176,1152]{1,0:T(8,128)(2,1)S(1)} %collective-permute-done.refs_3_, ...), custom_call_target="tpu_custom_call" | custom-call | flops 3774873600 | bytes 6225920 | tf_op jit(solution)/shard_map/weights/pallas_call | solution.py:173
  57.5 5.3 %collective-permute-done.17.refs_8_ = bf16[176,1152]{1,0:T(8,128)(2,1)S(1)} collective-permute-done((bf16[176,1152]{1,0:T(8,128)(2,1)S(1)}, bf16[176,1152]{1,0:T(8,128)(2,1)S(1)}, u32[]{:S(2)}, u32[]{:S(2)}) %collective-permute-start.17) | collective-permute-done | bytes 405536 | tf_op jit(solution)/shard_map/ppermute | solution.py:56
  62.8 5.2 %weights.3 = (bf16[1280,1152]{1,0:T(8,128)(2,1)S(1)}, bf16[1280,1280]{1,0:T(8,128)(2,1)S(1)}, bf16[640,1280]{1,0:T(8,128)(2,1)S(1)}) custom-call(f32[2]{0:T(128)S(1)} %pad_maximum_fusion.3.refs_0_, s32[1]{0:T(128)} %bitcast.2.refs_1_, bf16[176,1152]{1,0:T(8,128)(2,1)S(1)} %collective-permute-done.6.refs_2_, ...), custom_call_target="tpu_custom_call" | custom-call | flops 3774873600 | bytes 6225920 | tf_op jit(solution)/shard_map/weights/pallas_call | solution.py:173
  68.7 8.7 %text_terms.1 = (f32[304,1280]{1,0:T(8,128)S(1)}, bf16[304,1280]{1,0:T(8,128)(2,1)S(1)}, bf16[304,1280]{1,0:T(8,128)(2,1)S(1)}, bf16[144,1280]{1,0:T(8,128)(2,1)S(1)}, bf16[160,1280]{1,0:T(8,128)(2,1)S(1)}) custom-call(s32[8]{0:T(128)S(1)} %stack.44.place, bf16[1280,1152]{1,0:T(8,128)(2,1)S(1)} %get-tuple-element.59.image_a, ...), custom_call_target="tpu_custom_call" | custom-call | flops 7549747200 | bytes 6553600 | tf_op jit(solution)/shard_map/text_terms/pallas_call | solution.py:222
  77.5 2.0 %collective-permute-start.27 = (bf16[160,1280]{1,0:T(8,128)(2,1)S(1)}, bf16[160,1280]{1,0:T(8,128)(2,1)S(1)}, u32[]{:S(2)}, u32[]{:S(2)}) collective-permute-start(bf16[160,1280]{1,0:T(8,128)(2,1)S(1)} %get-tuple-element.84), channel_id=1, source_target_pairs={{0,96},{1,97},{16,112},{17,113},{2,98},{3,99},{18,114},{19,115},{4... | collective-permute-start | bytes 1228808 | tf_op jit(solution)/shard_map/ppermute | solution.py:56
  79.5 8.6 %image_terms.1 = (f32[320,1152]{1,0:T(8,128)S(1)}, bf16[320,1152]{1,0:T(8,128)(2,1)S(1)}, bf16[320,1152]{1,0:T(8,128)(2,1)S(1)}, bf16[160,1152]{1,0:T(8,128)(2,1)S(1)}, bf16[160,1152]{1,0:T(8,128)(2,1)S(1)}) custom-call(bf16[1280,1280]{1,0:T(8,128)(2,1)S(1)} %get-tuple-element.54.weight_a.refs_0_, bf16[640,1280]{1,0:T(8,128)(2,1)S(1)} %collective-permute-done.15.refs_1_, ...), custom_call_target="tpu_custom_call" | custom-call | flops 10000000000 | bytes 11796480 | tf_op jit(solution)/shard_map/image_terms/pallas_call | solution.py:259
  88.9 2.9 %collective-permute-start.22 = (bf16[160,1152]{1,0:T(8,128)(2,1)S(1)}, bf16[160,1152]{1,0:T(8,128)(2,1)S(1)}, u32[]{:S(2)}, u32[]{:S(2)}) collective-permute-start(bf16[160,1152]{1,0:T(8,128)(2,1)S(1)} %get-tuple-element.73), channel_id=1, source_target_pairs={{0,12},{1,13},{16,28},{17,29},{2,14},{3,15},{18,30},{19,31},{4,0},... | collective-permute-start | bytes 1105928 | tf_op jit(solution)/shard_map/ppermute | solution.py:56
  94.2 5.8 %collective-permute-done.20.refs_1_ = bf16[160,1152]{1,0:T(8,128)(2,1)S(1)} collective-permute-done((bf16[160,1152]{1,0:T(8,128)(2,1)S(1)}, bf16[160,1152]{1,0:T(8,128)(2,1)S(1)}, u32[]{:S(2)}, u32[]{:S(2)}) %collective-permute-start.20) | collective-permute-done | bytes 368672 | tf_op jit(solution)/shard_map/ppermute | solution.py:56
  100.3 3.3 %collective-permute-start.23 = (bf16[320,1152]{1,0:T(8,128)(2,1)S(1)}, bf16[320,1152]{1,0:T(8,128)(2,1)S(1)}, u32[]{:S(2)}, u32[]{:S(2)}) collective-permute-start(bf16[320,1152]{1,0:T(8,128)(2,1)S(1)} %add_rows.5), channel_id=1, source_target_pairs={{0,12},{1,13},{16,28},{17,29},{2,14},{3,15},{18,30},{19,31},{4,0},... | collective-permute-start | bytes 2211848 | tf_op jit(solution)/shard_map/ppermute | solution.py:56
  103.6 6.8 %collective-permute-done.26.ahead = bf16[304,1280]{1,0:T(8,128)(2,1)S(1)} collective-permute-done((bf16[304,1280]{1,0:T(8,128)(2,1)S(1)}, bf16[304,1280]{1,0:T(8,128)(2,1)S(1)}, u32[]{:S(2)}, u32[]{:S(2)}) %collective-permute-start.26) | collective-permute-done | bytes 778272 | tf_op jit(solution)/shard_map/ppermute | solution.py:56
  110.4 2.7 %collective-permute-done.28.back = bf16[304,1280]{1,0:T(8,128)(2,1)S(1)} collective-permute-done((bf16[304,1280]{1,0:T(8,128)(2,1)S(1)}, bf16[304,1280]{1,0:T(8,128)(2,1)S(1)}, u32[]{:S(2)}, u32[]{:S(2)}) %collective-permute-start.28) | collective-permute-done | bytes 778272 | tf_op jit(solution)/shard_map/ppermute | solution.py:56
  114.7 3.9 %collective-permute-done.21.ahead = bf16[320,1152]{1,0:T(8,128)(2,1)S(1)} collective-permute-done((bf16[320,1152]{1,0:T(8,128)(2,1)S(1)}, bf16[320,1152]{1,0:T(8,128)(2,1)S(1)}, u32[]{:S(2)}, u32[]{:S(2)}) %collective-permute-start.21) | collective-permute-done | bytes 737312 | tf_op jit(solution)/shard_map/ppermute | solution.py:56
  119.5 3.2 %collective-permute-start.24 = (bf16[160,1152]{1,0:T(8,128)(2,1)}, bf16[160,1152]{1,0:T(8,128)(2,1)}, u32[]{:S(2)}, u32[]{:S(2)}) collective-permute-start(bf16[160,1152]{1,0:T(8,128)(2,1)} %get-tuple-element.75), channel_id=1, source_target_pairs={{0,2},{1,3},{16,18},{17,19},{2,0},{3,1},{18,16},{19,17},{4,6},{5,7... | collective-permute-start | bytes 1105928 | tf_op jit(solution)/shard_map/ppermute | solution.py:56
  124.6 9.4 %collective-permute-done.24 = bf16[160,1152]{1,0:T(8,128)(2,1)} collective-permute-done((bf16[160,1152]{1,0:T(8,128)(2,1)}, bf16[160,1152]{1,0:T(8,128)(2,1)}, u32[]{:S(2)}, u32[]{:S(2)}) %collective-permute-start.24) | collective-permute-done | bytes 368672 | tf_op jit(solution)/shard_map/ppermute | solution.py:56
  135.2 2.0 %multiply_convert_fusion = bf16[160,1152]{1,0:T(8,128)(2,1)} fusion(bf16[160,1152]{1,0:T(8,128)(2,1)S(1)} %copy-done.1, f32[160,1152]{1,0:T(8,128)S(1)} %get-tuple-element.74, bf16[160,1152]{1,0:T(8,128)(2,1)} %collective-permute-done.24, f32[160]{0:T(256)S(1)} %multiply_reduce_fusion, f32[160]{0:T(256)S(1)} %reduce, f32[]{:T(128)} %bitcast), kind=kLoop, calls=%fused_computation.2 | loop fusion | flops 1658880 | bytes 1844484 | tf_op jit(solution)/shard_map/convert_element_type | solution.py:410
  (71 shorter events, 21.0 us)
Async XLA Ops:
  0.6 10.8 %collective-permute-start.5 = (bf16[144,1280]{1,0:T(8,128)(2,1)}, bf16[144,1280]{1,0:T(8,128)(2,1)S(1)}, u32[]{:S(2)}, u32[]{:S(2)}) collective-permute-start(bf16[144,1280]{1,0:T(8,128)(2,1)} %bitcast.15), channel_id=1, source_target_pairs={{0,16},{1,17},{16,0},{17,1},{2,18},{3,19},{18,2},{19,3},{4,20},{5,... | collective-permute-start | bytes 1105928 | tf_op jit(solution)/shard_map/ppermute | solution.py:56
  4.5 13.8 %collective-permute-start = (bf16[176,1152]{1,0:T(8,128)(2,1)S(1)}, bf16[176,1152]{1,0:T(8,128)(2,1)S(1)}, u32[]{:S(2)}, u32[]{:S(2)}) collective-permute-start(bf16[176,1152]{1,0:T(8,128)(2,1)S(1)} %get-tuple-element.46.refs_2_), channel_id=1, source_target_pairs={{0,4},{1,5},{16,20},{17,21},{2,6},{3,7},{18,22},{19,23},{4,8},{5,9... | collective-permute-start | bytes 1216520 | tf_op jit(solution)/shard_map/ppermute | solution.py:56
  6.1 13.8 %collective-permute-start.1 = (bf16[176,1152]{1,0:T(8,128)(2,1)S(1)}, bf16[176,1152]{1,0:T(8,128)(2,1)S(1)}, u32[]{:S(2)}, u32[]{:S(2)}) collective-permute-start(bf16[176,1152]{1,0:T(8,128)(2,1)S(1)} %get-tuple-element.46.refs_2_), channel_id=1, source_target_pairs={{0,12},{1,13},{16,28},{17,29},{2,14},{3,15},{18,30},{19,31},{4,0},... | collective-permute-start | bytes 1216520 | tf_op jit(solution)/shard_map/ppermute | solution.py:56
  12.5 19.8 %collective-permute-start.9 = (bf16[288,1280]{1,0:T(8,128)(2,1)S(1)}, bf16[288,1280]{1,0:T(8,128)(2,1)}, u32[]{:S(2)}, u32[]{:S(2)}) collective-permute-start(bf16[288,1280]{1,0:T(8,128)(2,1)S(1)} %pad_maximum_fusion.1.refs_0_), channel_id=1, source_target_pairs={{0,32},{1,33},{16,48},{17,49},{2,34},{3,35},{18,50},{19,51},{4,36}... | collective-permute-start | bytes 2211848 | tf_op jit(solution)/shard_map/ppermute | solution.py:56
  13.0 22.0 %collective-permute-start.10 = (bf16[288,1280]{1,0:T(8,128)(2,1)S(1)}, bf16[288,1280]{1,0:T(8,128)(2,1)}, u32[]{:S(2)}, u32[]{:S(2)}) collective-permute-start(bf16[288,1280]{1,0:T(8,128)(2,1)S(1)} %pad_maximum_fusion.1.refs_0_), channel_id=1, source_target_pairs={{0,96},{1,97},{16,112},{17,113},{2,98},{3,99},{18,114},{19,115},{4... | collective-permute-start | bytes 2211848 | tf_op jit(solution)/shard_map/ppermute | solution.py:56
  14.6 11.7 %collective-permute-start.6 = (bf16[176,1152]{1,0:T(8,128)(2,1)S(1)}, bf16[176,1152]{1,0:T(8,128)(2,1)S(1)}, u32[]{:S(2)}, u32[]{:S(2)}) collective-permute-start(bf16[176,1152]{1,0:T(8,128)(2,1)S(1)} %get-tuple-element.46.refs_2_), channel_id=1, source_target_pairs={{0,2},{1,3},{16,18},{17,19},{2,0},{3,1},{18,16},{19,17},{4,6},{5,7... | collective-permute-start | bytes 1216520 | tf_op jit(solution)/shard_map/ppermute | solution.py:56
  18.3 7.2 %collective-permute-start.2 = (bf16[96,1152]{1,0:T(8,128)(2,1)S(1)}, bf16[96,1152]{1,0:T(8,128)(2,1)S(1)}, u32[]{:S(2)}, u32[]{:S(2)}) collective-permute-start(bf16[96,1152]{1,0:T(8,128)(2,1)S(1)} %slice.24), channel_id=1, source_target_pairs={{0,4},{1,5},{16,20},{17,21},{2,6},{3,7},{18,22},{19,23},{4,8},{5,9... | collective-permute-start | bytes 663560 | tf_op jit(solution)/shard_map/ppermute | solution.py:56
  20.0 6.3 %collective-permute-start.3 = (bf16[80,1152]{1,0:T(8,128)(2,1)S(1)}, bf16[80,1152]{1,0:T(8,128)(2,1)S(1)}, u32[]{:S(2)}, u32[]{:S(2)}) collective-permute-start(bf16[80,1152]{1,0:T(8,128)(2,1)S(1)} %slice.25), channel_id=1, source_target_pairs={{0,12},{1,13},{16,28},{17,29},{2,14},{3,15},{18,30},{19,31},{4,0},... | collective-permute-start | bytes 552968 | tf_op jit(solution)/shard_map/ppermute | solution.py:56
  26.2 10.3 %collective-permute-start.7 = (bf16[176,1152]{1,0:T(8,128)(2,1)S(1)}, bf16[176,1152]{1,0:T(8,128)(2,1)S(1)}, u32[]{:S(2)}, u32[]{:S(2)}) collective-permute-start(bf16[176,1152]{1,0:T(8,128)(2,1)S(1)} %collective-permute-done.6.refs_2_), channel_id=1, source_target_pairs={{0,4},{1,5},{16,20},{17,21},{2,6},{3,7},{18,22},{19,23},{4,8},{5,9... | collective-permute-start | bytes 1216520 | tf_op jit(solution)/shard_map/ppermute | solution.py:56
  27.8 8.8 %collective-permute-start.8 = (bf16[176,1152]{1,0:T(8,128)(2,1)S(1)}, bf16[176,1152]{1,0:T(8,128)(2,1)S(1)}, u32[]{:S(2)}, u32[]{:S(2)}) collective-permute-start(bf16[176,1152]{1,0:T(8,128)(2,1)S(1)} %collective-permute-done.6.refs_2_), channel_id=1, source_target_pairs={{0,12},{1,13},{16,28},{17,29},{2,14},{3,15},{18,30},{19,31},{4,0},... | collective-permute-start | bytes 1216520 | tf_op jit(solution)/shard_map/ppermute | solution.py:56
  30.8 19.8 %collective-permute-start.4 = (bf16[704,1152]{1,0:T(8,128)(2,1)}, bf16[704,1152]{1,0:T(8,128)(2,1)}, u32[]{:S(2)}, u32[]{:S(2)}) collective-permute-start(bf16[704,1152]{1,0:T(8,128)(2,1)} %constant_dynamic-update-slice_fusion), channel_id=1, source_target_pairs={{0,1},{1,0},{16,17},{17,16},{2,3},{3,2},{18,19},{19,18},{4,5},{5,4... | collective-permute-start | bytes 4866056 | tf_op jit(solution)/shard_map/ppermute | solution.py:56
  33.3 11.1 %collective-permute-start.13 = (bf16[144,1280]{1,0:T(8,128)(2,1)S(1)}, bf16[144,1280]{1,0:T(8,128)(2,1)S(1)}, u32[]{:S(2)}, u32[]{:S(2)}) collective-permute-start(bf16[144,1280]{1,0:T(8,128)(2,1)S(1)} %slice.26), channel_id=1, source_target_pairs={{0,32},{1,33},{16,48},{17,49},{2,34},{3,35},{18,50},{19,51},{4,36}... | collective-permute-start | bytes 1105928 | tf_op jit(solution)/shard_map/ppermute | solution.py:56
  36.1 12.0 %collective-permute-start.14 = (bf16[144,1280]{1,0:T(8,128)(2,1)S(1)}, bf16[144,1280]{1,0:T(8,128)(2,1)S(1)}, u32[]{:S(2)}, u32[]{:S(2)}) collective-permute-start(bf16[144,1280]{1,0:T(8,128)(2,1)S(1)} %slice.27), channel_id=1, source_target_pairs={{0,96},{1,97},{16,112},{17,113},{2,98},{3,99},{18,114},{19,115},{4... | collective-permute-start | bytes 1105928 | tf_op jit(solution)/shard_map/ppermute | solution.py:56
  36.6 14.0 %collective-permute-start.11 = (bf16[96,1152]{1,0:T(8,128)(2,1)S(1)}, bf16[96,1152]{1,0:T(8,128)(2,1)S(1)}, u32[]{:S(2)}, u32[]{:S(2)}) collective-permute-start(bf16[96,1152]{1,0:T(8,128)(2,1)S(1)} %slice.20), channel_id=1, source_target_pairs={{0,4},{1,5},{16,20},{17,21},{2,6},{3,7},{18,22},{19,23},{4,8},{5,9... | collective-permute-start | bytes 663560 | tf_op jit(solution)/shard_map/ppermute | solution.py:56
  38.2 12.3 %collective-permute-start.12 = (bf16[80,1152]{1,0:T(8,128)(2,1)S(1)}, bf16[80,1152]{1,0:T(8,128)(2,1)S(1)}, u32[]{:S(2)}, u32[]{:S(2)}) collective-permute-start(bf16[80,1152]{1,0:T(8,128)(2,1)S(1)} %slice.21), channel_id=1, source_target_pairs={{0,12},{1,13},{16,28},{17,29},{2,14},{3,15},{18,30},{19,31},{4,0},... | collective-permute-start | bytes 552968 | tf_op jit(solution)/shard_map/ppermute | solution.py:56
  40.1 10.5 %copy-start.4 = (bf16[80,1152]{1,0:T(8,128)(2,1)S(1)}, bf16[80,1152]{1,0:T(8,128)(2,1)}, u32[]{:S(2)}) copy-start(bf16[80,1152]{1,0:T(8,128)(2,1)} %copy-done.3) | copy-start | bytes 552964
  44.4 18.5 %collective-permute-start.16 = (bf16[528,1152]{1,0:T(8,128)(2,1)S(1)}, bf16[528,1152]{1,0:T(8,128)(2,1)S(1)}, u32[]{:S(2)}, u32[]{:S(2)}) collective-permute-start(bf16[528,1152]{1,0:T(8,128)(2,1)S(1)} %pad_maximum_fusion), channel_id=1, source_target_pairs={{0,1},{1,0},{16,17},{17,16},{2,3},{3,2},{18,19},{19,18},{4,5},{5,4... | collective-permute-start | bytes 3649544 | tf_op jit(solution)/shard_map/ppermute | solution.py:56
  56.8 22.7 %collective-permute-start.19 = (bf16[1152,1280]{1,0:T(8,128)(2,1)S(1)}, bf16[1152,1280]{1,0:T(8,128)(2,1)S(1)}, u32[]{:S(2)}, u32[]{:S(2)}) collective-permute-start(bf16[1152,1280]{1,0:T(8,128)(2,1)S(1)} %get-tuple-element.68.refs_8_.refs_9_.refs_4_), channel_id=1, source_target_pairs={{0,1},{1,0},{16,17},{17,16},{2,3},{3,2},{18,19},{19,18},{4,5},{5,4... | collective-permute-start | bytes 8847368 | tf_op jit(solution)/shard_map/ppermute | solution.py:56
  56.9 5.9 %collective-permute-start.17 = (bf16[176,1152]{1,0:T(8,128)(2,1)S(1)}, bf16[176,1152]{1,0:T(8,128)(2,1)S(1)}, u32[]{:S(2)}, u32[]{:S(2)}) collective-permute-start(bf16[176,1152]{1,0:T(8,128)(2,1)S(1)} %pad_maximum_fusion.2), channel_id=1, source_target_pairs={{0,1},{1,0},{16,17},{17,16},{2,3},{3,2},{18,19},{19,18},{4,5},{5,4... | collective-permute-start | bytes 1216520 | tf_op jit(solution)/shard_map/ppermute | solution.py:56
  68.1 9.3 %collective-permute-start.18 = (bf16[640,1280]{1,0:T(8,128)(2,1)S(1)}, bf16[640,1280]{1,0:T(8,128)(2,1)S(1)}, u32[]{:S(2)}, u32[]{:S(2)}) collective-permute-start(bf16[640,1280]{1,0:T(8,128)(2,1)S(1)} %get-tuple-element.58), channel_id=1, source_target_pairs={{0,1},{1,0},{16,17},{17,16},{2,3},{3,2},{18,19},{19,18},{4,5},{5,4... | collective-permute-start | bytes 4915208 | tf_op jit(solution)/shard_map/ppermute | solution.py:56
  68.3 11.2 %collective-permute-start.15 = (bf16[640,1280]{1,0:T(8,128)(2,1)S(1)}, bf16[640,1280]{1,0:T(8,128)(2,1)S(1)}, u32[]{:S(2)}, u32[]{:S(2)}) collective-permute-start(bf16[640,1280]{1,0:T(8,128)(2,1)S(1)} %get-tuple-element.55), channel_id=1, source_target_pairs={{0,1},{1,0},{16,17},{17,16},{2,3},{3,2},{18,19},{19,18},{4,5},{5,4... | collective-permute-start | bytes 4915208 | tf_op jit(solution)/shard_map/ppermute | solution.py:56
  77.4 14.3 %collective-permute-start.25 = (bf16[144,1280]{1,0:T(8,128)(2,1)S(1)}, bf16[144,1280]{1,0:T(8,128)(2,1)S(1)}, u32[]{:S(2)}, u32[]{:S(2)}) collective-permute-start(bf16[144,1280]{1,0:T(8,128)(2,1)S(1)} %get-tuple-element.82), channel_id=1, source_target_pairs={{0,32},{1,33},{16,48},{17,49},{2,34},{3,35},{18,50},{19,51},{4,36}... | collective-permute-start | bytes 1105928 | tf_op jit(solution)/shard_map/ppermute | solution.py:56
  77.5 15.7 %collective-permute-start.27 = (bf16[160,1280]{1,0:T(8,128)(2,1)S(1)}, bf16[160,1280]{1,0:T(8,128)(2,1)S(1)}, u32[]{:S(2)}, u32[]{:S(2)}) collective-permute-start(bf16[160,1280]{1,0:T(8,128)(2,1)S(1)} %get-tuple-element.84), channel_id=1, source_target_pairs={{0,96},{1,97},{16,112},{17,113},{2,98},{3,99},{18,114},{19,115},{4... | collective-permute-start | bytes 1228808 | tf_op jit(solution)/shard_map/ppermute | solution.py:56
  88.2 11.8 %collective-permute-start.20 = (bf16[160,1152]{1,0:T(8,128)(2,1)S(1)}, bf16[160,1152]{1,0:T(8,128)(2,1)S(1)}, u32[]{:S(2)}, u32[]{:S(2)}) collective-permute-start(bf16[160,1152]{1,0:T(8,128)(2,1)S(1)} %get-tuple-element.71), channel_id=1, source_target_pairs={{0,4},{1,5},{16,20},{17,21},{2,6},{3,7},{18,22},{19,23},{4,8},{5,9... | collective-permute-start | bytes 1105928 | tf_op jit(solution)/shard_map/ppermute | solution.py:56
  88.9 11.3 %collective-permute-start.22 = (bf16[160,1152]{1,0:T(8,128)(2,1)S(1)}, bf16[160,1152]{1,0:T(8,128)(2,1)S(1)}, u32[]{:S(2)}, u32[]{:S(2)}) collective-permute-start(bf16[160,1152]{1,0:T(8,128)(2,1)S(1)} %get-tuple-element.73), channel_id=1, source_target_pairs={{0,12},{1,13},{16,28},{17,29},{2,14},{3,15},{18,30},{19,31},{4,0},... | collective-permute-start | bytes 1105928 | tf_op jit(solution)/shard_map/ppermute | solution.py:56
  91.9 18.5 %collective-permute-start.26 = (bf16[304,1280]{1,0:T(8,128)(2,1)S(1)}, bf16[304,1280]{1,0:T(8,128)(2,1)S(1)}, u32[]{:S(2)}, u32[]{:S(2)}) collective-permute-start(bf16[304,1280]{1,0:T(8,128)(2,1)S(1)} %add_rows.6), channel_id=1, source_target_pairs={{0,32},{1,33},{16,48},{17,49},{2,34},{3,35},{18,50},{19,51},{4,36}... | collective-permute-start | bytes 2334728 | tf_op jit(solution)/shard_map/ppermute | solution.py:56
  93.4 19.7 %collective-permute-start.28 = (bf16[304,1280]{1,0:T(8,128)(2,1)S(1)}, bf16[304,1280]{1,0:T(8,128)(2,1)S(1)}, u32[]{:S(2)}, u32[]{:S(2)}) collective-permute-start(bf16[304,1280]{1,0:T(8,128)(2,1)S(1)} %add_rows.7), channel_id=1, source_target_pairs={{0,96},{1,97},{16,112},{17,113},{2,98},{3,99},{18,114},{19,115},{4... | collective-permute-start | bytes 2334728 | tf_op jit(solution)/shard_map/ppermute | solution.py:56
  100.1 18.5 %collective-permute-start.21 = (bf16[320,1152]{1,0:T(8,128)(2,1)S(1)}, bf16[320,1152]{1,0:T(8,128)(2,1)S(1)}, u32[]{:S(2)}, u32[]{:S(2)}) collective-permute-start(bf16[320,1152]{1,0:T(8,128)(2,1)S(1)} %add_rows.4), channel_id=1, source_target_pairs={{0,4},{1,5},{16,20},{17,21},{2,6},{3,7},{18,22},{19,23},{4,8},{5,9... | collective-permute-start | bytes 2211848 | tf_op jit(solution)/shard_map/ppermute | solution.py:56
  100.3 18.3 %collective-permute-start.23 = (bf16[320,1152]{1,0:T(8,128)(2,1)S(1)}, bf16[320,1152]{1,0:T(8,128)(2,1)S(1)}, u32[]{:S(2)}, u32[]{:S(2)}) collective-permute-start(bf16[320,1152]{1,0:T(8,128)(2,1)S(1)} %add_rows.5), channel_id=1, source_target_pairs={{0,12},{1,13},{16,28},{17,29},{2,14},{3,15},{18,30},{19,31},{4,0},... | collective-permute-start | bytes 2211848 | tf_op jit(solution)/shard_map/ppermute | solution.py:56
  113.4 10.2 %collective-permute-start.29 = (bf16[160,1280]{1,0:T(8,128)(2,1)S(1)}, bf16[160,1280]{1,0:T(8,128)(2,1)S(1)}, u32[]{:S(2)}, u32[]{:S(2)}) collective-permute-start(bf16[160,1280]{1,0:T(8,128)(2,1)S(1)} %get-tuple-element.86.gave), channel_id=1, source_target_pairs={{0,16},{1,17},{16,0},{17,1},{2,18},{3,19},{18,2},{19,3},{4,20},{5,... | collective-permute-start | bytes 1228808 | tf_op jit(solution)/shard_map/ppermute | solution.py:56
  119.5 14.4 %copy-start.1 = (bf16[160,1152]{1,0:T(8,128)(2,1)S(1)}, bf16[160,1152]{1,0:T(8,128)(2,1)}, u32[]{:S(2)}) copy-start(bf16[160,1152]{1,0:T(8,128)(2,1)} %image.1) | copy-start | bytes 1105924
  119.5 14.4 %collective-permute-start.24 = (bf16[160,1152]{1,0:T(8,128)(2,1)}, bf16[160,1152]{1,0:T(8,128)(2,1)}, u32[]{:S(2)}, u32[]{:S(2)}) collective-permute-start(bf16[160,1152]{1,0:T(8,128)(2,1)} %get-tuple-element.75), channel_id=1, source_target_pairs={{0,2},{1,3},{16,18},{17,19},{2,0},{3,1},{18,16},{19,17},{4,6},{5,7... | collective-permute-start | bytes 1105928 | tf_op jit(solution)/shard_map/ppermute | solution.py:56
  (3 other events, 11.9 us)

commit v3 on v2

--- a/solution.py
+++ b/solution.py
@@ -76,14 +76,15 @@
     out[:half, :] = unit[:half]
     out[half + TAIL :, :] = unit[half:]
     index = pairs[...]
-    kind = lax.broadcasted_iota(jnp.int32, (TAIL, width), 0)
+    kind = lax.broadcasted_iota(jnp.int32, (TAIL, rows), 0)
     part = jnp.where(kind == 0, index >> 8, jnp.where(kind == 1, index & 255, 0))
-    out[half : half + TAIL, :] = part.astype(F32).astype(BF16)
+    out[half : half + TAIL, :] = jnp.zeros((TAIL, width), BF16)
+    out[half : half + TAIL, :rows] = part.astype(F32).astype(BF16)
 
 
 def image_units(image, pairs):
     rows, width = image.shape
-    pairs = jnp.pad(pairs[None], ((0, 0), (0, width - rows)))
+    pairs = pairs[None]
     return pl.pallas_call(
         unit_kernel,
         out_shape=[
@@ -127,7 +128,7 @@
         in_specs=[SMEM] + [VMEM] * len(pieces),
         out_specs=[VMEM] * 3,
         compiler_params=params(12),
-        cost_estimate=cost(10_000_000_000, 32 * depth * width),
+        cost_estimate=cost(40_000_000_000, 32 * depth * width),
         name="text_units",
     )(place, *pieces)
 
@@ -180,13 +181,13 @@
         in_specs=[SMEM, SMEM] + [VMEM] * (len(pieces) + 1),
         out_specs=[VMEM] * 3,
         compiler_params=params(12),
-        cost_estimate=cost(2 * count * width * columns, 2 * count * (width + columns)),
+        cost_estimate=cost(8_000_000_000, 2 * count * (width + columns)),
         name="weights",
     )(scalars, first_text, *pieces, text)
 
 
 def text_back_kernel(place, image_a, weight_a, image_b, weight_b, raw, *refs):
-    outs, back = refs[:5], refs[5]
+    outs, back = refs[:8], refs[8]
     width, columns = back.shape
     block = 384
     dots = jnp.zeros((1, columns), F32)
@@ -200,36 +201,28 @@
         dots += jnp.sum(part * raw[f : f + block, :].astype(F32), axis=0, keepdims=True)
     tail = split3(dots)
     empty = jnp.zeros((1, columns), F32)
-    depth = width // 4
+    depth = width // 8
     for i in range(4):
-        start = pl.multiple_of(place[2 * i] // 2 * depth, 8)
+        for h in range(2):
+            out = outs[2 * i + h]
+            start = pl.multiple_of(place[2 * i + h] * depth, 16)
+            out[:depth, :] = back[pl.ds(start, depth), :].astype(out.dtype)
         spread = [empty] * 3 * i + list(tail) + [empty] * (TAIL - 3 * i - 3)
-        spread = jnp.concatenate(spread, 0)
-        if i < 3:
-            outs[i][:depth, :] = back[pl.ds(start, depth), :].astype(outs[i].dtype)
-            outs[i][depth:, :] = spread.astype(outs[i].dtype)
-        else:
-            half = depth // 2
-            outs[3][...] = back[pl.ds(start, half), :].astype(BF16)
-            outs[4][:half, :] = back[pl.ds(start + half, half), :].astype(BF16)
-            outs[4][half:, :] = spread.astype(BF16)
+        out[depth:, :] = jnp.concatenate(spread, 0).astype(out.dtype)
 
 
 def text_terms(place, image_a, weight_a, image_b, weight_b, raw):
     count, width = image_a.shape
     columns = weight_a.shape[1]
-    shape = (width // 4 + TAIL, columns)
     return pl.pallas_call(
         text_back_kernel,
         out_shape=[
-            jax.ShapeDtypeStruct(shape, F32),
-            jax.ShapeDtypeStruct(shape, BF16),
-            jax.ShapeDtypeStruct(shape, BF16),
-            jax.ShapeDtypeStruct((width // 8, columns), BF16),
-            jax.ShapeDtypeStruct((width // 8 + TAIL, columns), BF16),
+            jax.ShapeDtypeStruct((width // 8 + h * TAIL, columns), BF16 if i else F32)
+            for i in range(4)
+            for h in range(2)
         ],
         in_specs=[SMEM] + [VMEM] * 5,
-        out_specs=[VMEM] * 5,
+        out_specs=[VMEM] * 8,
         scratch_shapes=[pltpu.VMEM((width, columns), F32)],
         compiler_params=params(16),
         cost_estimate=cost(4 * count * width * columns, 4 * count * columns),
@@ -245,22 +238,17 @@
                 own[block, :], text[...], NT, preferred_element_type=F32
             ) + lax.dot_general(got[block, :], text_got[...], NT, preferred_element_type=F32)
             for k in range(2):
-                i = start + k
-                mine = back[k * rows : (k + 1) * rows]
-                if i == 3:
-                    outs[3 + h][...] = mine.astype(BF16)
-                else:
-                    outs[i][h * rows : (h + 1) * rows, :] = mine.astype(outs[i].dtype)
+                out = outs[2 * (start + k) + h]
+                out[...] = back[k * rows : (k + 1) * rows].astype(out.dtype)
 
 
 def image_terms(rows, own_a, got_a, own_b, got_b, text, text_got):
     width, columns = text.shape
-    kinds = [(2 * rows, F32), (2 * rows, BF16), (2 * rows, BF16), (rows, BF16), (rows, BF16)]
     return pl.pallas_call(
         lambda *refs: image_back_kernel(rows, *refs),
-        out_shape=[jax.ShapeDtypeStruct((count, width), kind) for count, kind in kinds],
+        out_shape=[jax.ShapeDtypeStruct((rows, width), F32 if i < 2 else BF16) for i in range(8)],
         in_specs=[VMEM] * 6,
-        out_specs=[VMEM] * 5,
+        out_specs=[VMEM] * 8,
         compiler_params=params(16),
         cost_estimate=cost(10_000_000_000, 8 * width * columns),
         name="image_terms",
@@ -285,69 +273,84 @@
         in_specs=[VMEM] * 2,
         out_specs=VMEM,
         compiler_params=params(8),
-        cost_estimate=cost(0, 6 * value.size),
+        cost_estimate=cost(5_000_000_000, 6 * value.size),
         name="add_rows",
     )(value, more)
 
 
-def ring_terms(parts, far, axis):
-    far = [send(far[0], (axis, 1)), send(far[1], (axis, -1))]
-    ahead = add_rows(parts[2], far[0], 0)
-    back = add_rows(parts[1], far[1], far[0].shape[0])
-    return parts[0], send(ahead, (axis, 1)), send(back, (axis, -1))
-
-
-def halves_kernel(which, own, ahead, back, keep, give):
-    size = keep.shape[0]
-    rest = own.shape[0] - 2 * size
-    mine = pl.multiple_of(which[0] * size, 16)
-    other = pl.multiple_of((1 - which[0]) * size, 16)
-
-    def total(rows):
-        return own[rows, :] + ahead[rows, :].astype(F32) + back[rows, :].astype(F32)
-
-    keep[...] = total(pl.ds(mine, size))
-    give[:size, :] = total(pl.ds(other, size)).astype(BF16)
-    if rest:
-        give[size:, :] = total(pl.ds(2 * size, rest)).astype(BF16)
-
-
-def sum_halves(which, own, ahead, back, size):
-    rows, width = own.shape
-    return pl.pallas_call(
-        halves_kernel,
-        out_shape=[
-            jax.ShapeDtypeStruct((size, width), F32),
-            jax.ShapeDtypeStruct((rows - size, width), BF16),
-        ],
-        in_specs=[SMEM] + [VMEM] * 3,
-        out_specs=[VMEM] * 2,
+def hold_kernel(value, *refs):
+    refs[-1][...] = value[...]
+
+
+def hold(value, *others):
+    return pl.pallas_call(
+        hold_kernel,
+        out_shape=jax.ShapeDtypeStruct(value.shape, value.dtype),
+        in_specs=[VMEM] + [pl.BlockSpec(memory_space=pl.ANY)] * len(others),
+        out_specs=VMEM,
+        compiler_params=params(4),
+        cost_estimate=cost(20_000_000_000, 0),
+        name="hold",
+    )(value, *others)
+
+
+def add_three_kernel(own, ahead, back, out):
+    out[...] = (own[...] + ahead[...].astype(F32) + back[...].astype(F32)).astype(BF16)
+
+
+def add_three(own, ahead, back):
+    return pl.pallas_call(
+        add_three_kernel,
+        out_shape=jax.ShapeDtypeStruct(own.shape, BF16),
+        in_specs=[VMEM] * 3,
+        out_specs=VMEM,
         compiler_params=params(8),
-        cost_estimate=cost(0, 12 * own.size),
-        name="sum_halves",
-    )(which, own, ahead, back)
-
-
-def text_final_kernel(temper, keep, gave, given, raw, inverse, out):
+        cost_estimate=cost(0, 10 * own.size),
+        name="add_three",
+    )(own, ahead, back)
+
+
+def image_final_kernel(temper, own, ahead, back, given, image, inverse, out):
+    total = own[...] + ahead[...].astype(F32) + back[...].astype(F32) + given[...].astype(F32)
+    scale = inverse[...]
+    unit = image[...].astype(F32) * scale
+    dot = jnp.sum(unit * total, axis=1, keepdims=True)
+    out[...] = (temper[0] * (total - unit * dot) * scale).astype(BF16)
+
+
+def image_final(temper, own, ahead, back, given, image, inverse):
+    return pl.pallas_call(
+        image_final_kernel,
+        out_shape=jax.ShapeDtypeStruct(image.shape, BF16),
+        in_specs=[SMEM] + [VMEM] * 6,
+        out_specs=VMEM,
+        compiler_params=params(8),
+        cost_estimate=cost(0, 16 * image.size),
+        name="image_final",
+    )(temper, own, ahead, back, given, image, inverse)
+
+
+def text_final_kernel(temper, own, ahead, back, gave, given, raw, inverse, out):
     depth = raw.shape[0]
     scale = inverse[...]
-    back = keep[...] + given[:depth, :].astype(F32)
+    total = own[...] + ahead[...].astype(F32) + back[...].astype(F32)
+    total += given[:depth, :].astype(F32)
     tails = gave[depth:, :].astype(F32) + given[depth:, :].astype(F32)
     dots = jnp.sum(tails, axis=0, keepdims=True) * scale
     unit = raw[...].astype(F32) * scale
-    out[...] = (temper[0] * (back - unit * dots) * scale).astype(BF16)
-
-
-def text_final(temper, keep, gave, given, raw, inverse):
+    out[...] = (temper[0] * (total - unit * dots) * scale).astype(BF16)
+
+
+def text_final(temper, own, ahead, back, gave, given, raw, inverse):
     return pl.pallas_call(
         text_final_kernel,
         out_shape=jax.ShapeDtypeStruct(raw.shape, BF16),
-        in_specs=[SMEM] + [VMEM] * 5,
+        in_specs=[SMEM] + [VMEM] * 7,
         out_specs=VMEM,
         compiler_params=params(8),
-        cost_estimate=cost(0, 12 * raw.size),
+        cost_estimate=cost(0, 16 * raw.size),
         name="text_final",
-    )(temper, keep, gave, given, raw, inverse)
+    )(temper, own, ahead, back, gave, given, raw, inverse)
 
 
 def local(image, text, pair_text, log_scale, bias):
@@ -361,53 +364,73 @@
 
     own_text = text.T
     text_lo = send(own_text, "lo")
+    text_a, text_b = send(own_text, ("x", 1)), send(own_text, ("x", -1))
     unit, image_inverse = image_units(image, pair_text)
     a, b = send(unit, ("y", 1)), send(unit, ("y", -1))
-    text2 = jnp.concatenate([own_text, text_lo], 0)
-    text_a, text_b = send(text2, ("x", 1)), send(text2, ("x", -1))
-    unit_hi = send(after(unit, text_lo), "hi")
+    unit_hi = send(hold(unit, text_lo), "hi")
+    text_c, text_a = lax.optimization_barrier((text_lo, text_a))
+    text_c = send(text_c, ("x", 1))
+    text_d, text_b = lax.optimization_barrier((text_lo, text_b))
+    text_d = send(text_d, ("x", -1))
+    text_a2 = send(text_a, ("x", 1))
+    a2 = send(a, ("y", 1))
     cut = rows // 2 + TAIL
-    a2, b2 = send(a[:cut], ("y", 1)), send(b[cut:], ("y", -1))
-    unit_hi = after(unit_hi, a2, b2)
-    c, d = send(unit_hi, ("y", 1)), send(unit_hi, ("y", -1))
-    text_a2, text_b2 = send(text_a[:depth], ("x", 1)), send(text_b[depth:], ("x", -1))
-    c, d, text_a, text_b = lax.optimization_barrier((c, d, text_a, text_b))
+    c = send(unit_hi, ("y", 1))
+    d, b = lax.optimization_barrier((unit_hi, b))
+    d = send(d, ("y", -1))
+    text_d2 = send(text_d, ("x", -1))
+    c, d, text_c, text_d = lax.optimization_barrier((c, d, text_c, text_d))
     c2, d2 = send(c[:cut], ("y", 1)), send(d[cut:], ("y", -1))
-    near, partner = [unit, a, b, a2, b2], [unit_hi, c, d, c2, d2]
+    near, partner = [unit, a, b, a2], [unit_hi, c, d, c2, d2]
     near.append(after(send(jnp.concatenate(near, 0), "core"), c2, d2))
     partner += [
         send(jnp.concatenate(partner[:3], 0), "core"),
         send(jnp.concatenate(partner[3:], 0), "core"),
     ]
-    text_pieces = [text2, text_a, text_b, text_a2, text_b2]
+    text_pieces = [own_text, text_lo, text_a, text_c, text_b, text_d, text_a2, text_d2]
 
     text_unit, text_raw, text_inverse = text_units(place, text_pieces, depth)
     image_a, weight_a, other_a = weights(scalars, first_text, near, rows, text_unit)
     got_a = send(other_a, "core")
-    text_got = send(after(text_unit, other_a), "core")
     image_b, weight_b, other_b = weights(
         after(scalars, other_a), first_text, partner, rows, text_unit
     )
     got_b = send(other_b, "core")
-    *text_parts, far0, far1 = text_terms(place, image_a, weight_a, image_b, weight_b, text_raw)
-    got_b, far0, far1, *text_parts = lax.optimization_barrier((got_b, far0, far1, *text_parts))
-    *image_parts, image_far0, image_far1 = image_terms(
-        rows, weight_a, got_a, weight_b, got_b, text_unit, text_got
+    text_got = send(after(text_unit, other_b), "core")
+    text_parts = text_terms(place, image_a, weight_a, image_b, weight_b, text_raw)
+    got_b, *text_parts = lax.optimization_barrier((got_b, *text_parts))
+    image_parts = image_terms(rows, weight_a, got_a, weight_b, got_b, text_unit, text_got)
+
+    x_own, x_back, x_ahead, x_far = [text_parts[2 * i : 2 * i + 2] for i in range(4)]
+    y_own, y_back, y_ahead, y_far = [image_parts[2 * i : 2 * i + 2] for i in range(4)]
+
+    x_relay1, x_relay0 = send(x_far[1], ("x", -1)), send(x_far[0], ("x", 1))
+    x_ahead1 = send(x_ahead[1], ("x", 1))
+    y_relay1, y_relay0 = send(y_far[1], ("y", -1)), send(y_far[0], ("y", 1))
+    x_back0, x_back1, x_ahead0, _ = lax.optimization_barrier((*x_back, x_ahead[0], y_own[0]))
+    x_back1, x_ahead0 = add_rows(x_back1, x_relay1, 0), add_rows(x_ahead0, x_relay0, 0)
+    x_ahead0, y_back0, y_back1, y_ahead0, y_ahead1 = lax.optimization_barrier(
+        (x_ahead0, *y_back, *y_ahead)
     )
-
-    *text_parts, _ = lax.optimization_barrier((*text_parts, image_parts[1]))
-    text_terms_here = ring_terms(text_parts, (far0, far1), "x")
-    image_terms_here = ring_terms(image_parts, (image_far0, image_far1), "y")
-    keep, gave = sum_halves(lo[None], *text_terms_here, depth)
-    given = send(gave, "lo")
-    grad_text = text_final(temper[None], keep, gave, given, own_text, text_inverse).T
-
-    keep, gave = sum_halves(jnp.zeros((1,), jnp.int32), *image_terms_here, rows)
-    image_back = keep + send(gave, "hi").astype(F32)
-    image_dir = image.astype(F32) * image_inverse
-    dot = jnp.sum(image_dir * image_back, axis=-1, keepdims=True)
-    grad_image = temper * (image_back - image_dir * dot) * image_inverse
-    return grad_image.astype(BF16), grad_text
+    x_back1, x_ahead0 = send(x_back1, ("x", -1)), send(x_ahead0, ("x", 1))
+    y_back1 = add_rows(y_back1, y_relay1, 0)
+    y_back1, y_ahead1, x_back0 = lax.optimization_barrier((y_back1, y_ahead1, x_back0))
+    y_back1, y_ahead1 = send(y_back1, ("y", -1)), send(y_ahead1, ("y", 1))
+    x_gave = add_three(x_own[1], x_ahead1, x_back1)
+    x_given = send(x_gave, "lo")
+    x_back0 = send(x_back0, ("x", -1))
+    y_ahead0, y_back0 = lax.optimization_barrier((add_rows(y_ahead0, y_relay0, 0), y_back0))
+    y_ahead0, y_back0 = send(y_ahead0, ("y", 1)), send(y_back0, ("y", -1))
+    y_given = send(add_three(y_own[1], y_ahead1, y_back1), "hi")
+
+    grad_text = text_final(
+        temper[None], x_own[0], x_ahead0, x_back0, x_gave, x_given, own_text, text_inverse
+    )
+    y_given, grad_text = lax.optimization_barrier((y_given, grad_text))
+    grad_image = image_final(
+        temper[None], y_own[0], y_ahead0, y_back0, y_given, image, image_inverse
+    )
+    return grad_image, grad_text.T
 
 
 def solution(mesh):

time: 138 us -> 118 us (0.86)
  waiting for transfers between devices: 47.7 us -> 35.7 us
  local copies, waits for them, and re-layouts: 8.31 us -> 2.54 us
  other arithmetic: 4.64 us -> 0.33 us
  starting transfers between devices: 40.3 us -> 43.2 us
    ppermute x30 -> x35, waiting for transfers between devices: 47.7 us -> 35.7 us  [send(): return lax.ppermute(value, AXES, MOVES[move])]
    ppermute x30 -> x35, starting transfers between devices: 40.3 us -> 43.2 us  [send(): return lax.ppermute(value, AXES, MOVES[move])]
    unnamed x14 -> x12, local copies, waits for them, and re-layouts: 4.75 us -> 2.42 us
    slice x4 -> x0, local copies, waits for them, and re-layouts: 2.06 us -> none  [the longest x1 1.02 us: local(): text_a[:depth]]
    convert_element_type x1 -> x0, other arithmetic: 2.03 us -> none  [local(): return (grad_image.astype(BF16), grad_text)]
    pallas_call x3 -> x5, Pallas kernels: 9.88 us -> 10.1 us  [the longest x1 8.72 us: text_terms(): pl.pallas_call(text_back_kernel, out_shape=[jax.ShapeDtypeStruct((width /...]
  transfers between devices with their start and end apart: 30 -> 35, of which waited for: 11 -> 12; matrix products, arithmetic and copies ran while one was open for 6% -> 0% of each run, Pallas kernels for 25% -> 23%
where the time goes in v3:
time: 118 us
  starting transfers between devices  43.2 us (37%)
  waiting for transfers between devices  35.7 us (30%)
  Pallas kernels  33.8 us (29%)
  local copies, waits for them, and re-layouts  2.54 us (2%)
  between operations  2.22 us (2%)
    ppermute x35, starting transfers between devices, send(): return lax.ppermute(value, AXES, MOVES[move])  43.2 us
    ppermute x35, waiting for transfers between devices, send(): return lax.ppermute(value, AXES, MOVES[move])  35.7 us
    pallas_call x2, Pallas kernels, weights(): pl.pallas_call(lambda *refs: weight_kernel(rows, *refs), out_shape=[jax.S...  11.1 us
    pallas_call x1, Pallas kernels, text_terms(): pl.pallas_call(text_back_kernel, out_shape=[jax.ShapeDtypeStruct((width /...  8.72 us
    pallas_call x1, Pallas kernels, image_terms(): pl.pallas_call(lambda *refs: image_back_kernel(rows, *refs), out_shape=[j...  8.65 us
    unnamed x12, local copies, waits for them, and re-layouts  2.42 us
  transfers between devices with their start and end apart: 35, of which 12 were waited for; matrix products, arithmetic and copies ran while one was open for 0% of the time, Pallas kernels for 23%

profile of v3, /device:TPU:6, one launch (start us, length us, event | category | flops | bytes accessed | tf_op | source)
XLA Modules:
  0.0 117.8 jit_solution(7296944377485918719)
XLA Ops:
  0.6 2.0 %collective-permute-start.1 = (bf16[144,1280]{1,0:T(8,128)(2,1)}, bf16[144,1280]{1,0:T(8,128)(2,1)S(1)}, u32[]{:S(2)}, u32[]{:S(2)}) collective-permute-start(bf16[144,1280]{1,0:T(8,128)(2,1)} %bitcast.12), channel_id=1, source_target_pairs={{0,16},{1,17},{16,0},{17,1},{2,18},{3,19},{18,2},{19,3},{4,20},{5,... | collective-permute-start | bytes 1105928 | tf_op jit(solution)/shard_map/ppermute | solution.py:56
  5.3 3.1 %collective-permute-start.3 = (bf16[176,1152]{1,0:T(8,128)(2,1)S(1)}, bf16[176,1152]{1,0:T(8,128)(2,1)S(1)}, u32[]{:S(2)}, u32[]{:S(2)}) collective-permute-start(bf16[176,1152]{1,0:T(8,128)(2,1)S(1)} %get-tuple-element.66.value.refs_2_), channel_id=1, source_target_pairs={{0,12},{1,13},{16,28},{17,29},{2,14},{3,15},{18,30},{19,31},{4,0},... | collective-permute-start | bytes 1216520 | tf_op jit(solution)/shard_map/ppermute | solution.py:56
  8.4 3.0 %collective-permute-done.1.refs_0_.refs_1_ = bf16[144,1280]{1,0:T(8,128)(2,1)S(1)} collective-permute-done((bf16[144,1280]{1,0:T(8,128)(2,1)}, bf16[144,1280]{1,0:T(8,128)(2,1)S(1)}, u32[]{:S(2)}, u32[]{:S(2)}) %collective-permute-start.1) | collective-permute-done | bytes 368672 | tf_op jit(solution)/shard_map/ppermute | solution.py:56
  11.5 3.8 %collective-permute-start.2 = (bf16[176,1152]{1,0:T(8,128)(2,1)S(1)}, bf16[176,1152]{1,0:T(8,128)(2,1)S(1)}, u32[]{:S(2)}, u32[]{:S(2)}) collective-permute-start(bf16[176,1152]{1,0:T(8,128)(2,1)S(1)} %hold.1), channel_id=1, source_target_pairs={{0,2},{1,3},{16,18},{17,19},{2,0},{3,1},{18,16},{19,17},{4,6},{5,7... | collective-permute-start | bytes 1216520 | tf_op jit(solution)/shard_map/ppermute | solution.py:56
  15.7 4.2 %collective-permute-done.refs_3_ = bf16[176,1152]{1,0:T(8,128)(2,1)S(1)} collective-permute-done((bf16[176,1152]{1,0:T(8,128)(2,1)S(1)}, bf16[176,1152]{1,0:T(8,128)(2,1)S(1)}, u32[]{:S(2)}, u32[]{:S(2)}) %collective-permute-start) | collective-permute-done | bytes 405536 | tf_op jit(solution)/shard_map/ppermute | solution.py:56
  22.6 1.9 %collective-permute-done.8.refs_2_ = bf16[144,1280]{1,0:T(8,128)(2,1)} collective-permute-done((bf16[144,1280]{1,0:T(8,128)(2,1)S(1)}, bf16[144,1280]{1,0:T(8,128)(2,1)}, u32[]{:S(2)}, u32[]{:S(2)}) %collective-permute-start.8) | collective-permute-done | bytes 368672 | tf_op jit(solution)/shard_map/ppermute | solution.py:56
  24.5 1.7 %collective-permute-start.9 = (bf16[144,1280]{1,0:T(8,128)(2,1)S(1)}, bf16[144,1280]{1,0:T(8,128)(2,1)S(1)}, u32[]{:S(2)}, u32[]{:S(2)}) collective-permute-start(bf16[144,1280]{1,0:T(8,128)(2,1)S(1)} %collective-permute-done.1.refs_0_.refs_1_), channel_id=1, source_target_pairs={{0,32},{1,33},{16,48},{17,49},{2,34},{3,35},{18,50},{19,51},{4,36}... | collective-permute-start | bytes 1105928 | tf_op jit(solution)/shard_map/ppermute | solution.py:56
  26.2 3.0 %collective-permute-start.7 = (bf16[176,1152]{1,0:T(8,128)(2,1)S(1)}, bf16[176,1152]{1,0:T(8,128)(2,1)S(1)}, u32[]{:S(2)}, u32[]{:S(2)}) collective-permute-start(bf16[176,1152]{1,0:T(8,128)(2,1)S(1)} %collective-permute-done.2.refs_2_), channel_id=1, source_target_pairs={{0,12},{1,13},{16,28},{17,29},{2,14},{3,15},{18,30},{19,31},{4,0},... | collective-permute-start | bytes 1216520 | tf_op jit(solution)/shard_map/ppermute | solution.py:56
  29.3 1.2 %collective-permute-done.11.refs_5_ = bf16[144,1280]{1,0:T(8,128)(2,1)} collective-permute-done((bf16[144,1280]{1,0:T(8,128)(2,1)S(1)}, bf16[144,1280]{1,0:T(8,128)(2,1)}, u32[]{:S(2)}, u32[]{:S(2)}) %collective-permute-start.11) | collective-permute-done | bytes 368672 | tf_op jit(solution)/shard_map/ppermute | solution.py:56
  30.5 1.2 %collective-permute-start.14 = (bf16[144,1280]{1,0:T(8,128)(2,1)}, bf16[144,1280]{1,0:T(8,128)(2,1)S(1)}, u32[]{:S(2)}, u32[]{:S(2)}) collective-permute-start(bf16[144,1280]{1,0:T(8,128)(2,1)} %collective-permute-done.8.refs_2_), channel_id=1, source_target_pairs={{0,32},{1,33},{16,48},{17,49},{2,34},{3,35},{18,50},{19,51},{4,36}... | collective-permute-start | bytes 1105928 | tf_op jit(solution)/shard_map/ppermute | solution.py:56
  32.7 2.3 %collective-permute-done.9.refs_3_ = bf16[144,1280]{1,0:T(8,128)(2,1)S(1)} collective-permute-done((bf16[144,1280]{1,0:T(8,128)(2,1)S(1)}, bf16[144,1280]{1,0:T(8,128)(2,1)S(1)}, u32[]{:S(2)}, u32[]{:S(2)}) %collective-permute-start.9) | collective-permute-done | bytes 368672 | tf_op jit(solution)/shard_map/ppermute | solution.py:56
  35.0 4.1 %collective-permute-done.6.refs_3_ = bf16[176,1152]{1,0:T(8,128)(2,1)S(1)} collective-permute-done((bf16[176,1152]{1,0:T(8,128)(2,1)S(1)}, bf16[176,1152]{1,0:T(8,128)(2,1)S(1)}, u32[]{:S(2)}, u32[]{:S(2)}) %collective-permute-start.6) | collective-permute-done | bytes 405536 | tf_op jit(solution)/shard_map/ppermute | solution.py:56
  39.3 2.0 %collective-permute-start.12 = (bf16[96,1152]{1,0:T(8,128)(2,1)S(1)}, bf16[96,1152]{1,0:T(8,128)(2,1)S(1)}, u32[]{:S(2)}, u32[]{:S(2)}) collective-permute-start(bf16[96,1152]{1,0:T(8,128)(2,1)S(1)} %slice.6), channel_id=1, source_target_pairs={{0,4},{1,5},{16,20},{17,21},{2,6},{3,7},{18,22},{19,23},{4,8},{5,9... | collective-permute-start | bytes 663560 | tf_op jit(solution)/shard_map/ppermute | solution.py:56
  41.6 2.3 %text_units.1 = (bf16[1152,1280]{1,0:T(8,128)(2,1)S(1)}, bf16[1152,1280]{1,0:T(8,128)(2,1)S(1)}, f32[1,1280]{1,0:T(1,128)S(1)}) custom-call(s32[8]{0:T(128)S(1)} %stack.41.place, bf16[144,1280]{1,0:T(8,128)(2,1)S(1)} %bitcast.15, bf16[144,1280]{1,0:T(8,128)(2,1)S(1)} %collective-permute-done.1.refs_0_.refs_1_, ...), custom_call_target="tpu_custom_call" | custom-call | flops 40000000000 | bytes 5898240 | tf_op jit(solution)/shard_map/text_units/pallas_call | solution.py:125
  44.8 2.6 %collective-permute-done.12.refs_5_ = bf16[96,1152]{1,0:T(8,128)(2,1)S(1)} collective-permute-done((bf16[96,1152]{1,0:T(8,128)(2,1)S(1)}, bf16[96,1152]{1,0:T(8,128)(2,1)S(1)}, u32[]{:S(2)}, u32[]{:S(2)}) %collective-permute-start.12) | collective-permute-done | bytes 221216 | tf_op jit(solution)/shard_map/ppermute | solution.py:56
  47.7 5.5 %weights.2 = (bf16[1280,1152]{1,0:T(8,128)(2,1)S(1)}, bf16[1280,1280]{1,0:T(8,128)(2,1)S(1)}, bf16[640,1280]{1,0:T(8,128)(2,1)S(1)}) custom-call(f32[2]{0:T(128)S(1)} %pad_maximum_fusion.3.refs_0_, s32[1]{0:T(128)} %bitcast.refs_1_, bf16[176,1152]{1,0:T(8,128)(2,1)S(1)} %get-tuple-element.66.value.refs_2_, ...), custom_call_target="tpu_custom_call" | custom-call | flops 8000000000 | bytes 6225920 | tf_op jit(solution)/shard_map/weights/pallas_call | solution.py:174
  53.2 5.6 %weights.3 = (bf16[1280,1152]{1,0:T(8,128)(2,1)S(1)}, bf16[1280,1280]{1,0:T(8,128)(2,1)S(1)}, bf16[640,1280]{1,0:T(8,128)(2,1)S(1)}) custom-call(f32[2]{0:T(128)S(1)} %pad_maximum_fusion.3.refs_0_, s32[1]{0:T(128)} %bitcast.refs_1_, bf16[176,1152]{1,0:T(8,128)(2,1)S(1)} %collective-permute-done.2.refs_2_, ...), custom_call_target="tpu_custom_call" | custom-call | flops 8000000000 | bytes 6225920 | tf_op jit(solution)/shard_map/weights/pallas_call | solution.py:174
  59.9 8.7 %text_terms.1 = (f32[144,1280]{1,0:T(8,128)S(1)}, f32[160,1280]{1,0:T(8,128)S(1)}, bf16[144,1280]{1,0:T(8,128)(2,1)S(1)}, bf16[160,1280]{1,0:T(8,128)(2,1)S(1)},...) custom-call(s32[8]{0:T(128)S(1)} %stack.41.place, ...), custom_call_target="tpu_custom_call" | custom-call | flops 7549747200 | bytes 6553600 | tf_op jit(solution)/shard_map/text_terms/pallas_call | solution.py:217
  68.6 3.5 %collective-permute-start.21 = (bf16[144,1280]{1,0:T(8,128)(2,1)S(1)}, bf16[144,1280]{1,0:T(8,128)(2,1)S(1)}, u32[]{:S(2)}, u32[]{:S(2)}) collective-permute-start(bf16[144,1280]{1,0:T(8,128)(2,1)S(1)} %get-tuple-element.102), channel_id=1, source_target_pairs={{0,32},{1,33},{16,48},{17,49},{2,34},{3,35},{18,50},{19,51},{4,36}... | collective-permute-start | bytes 1105928 | tf_op jit(solution)/shard_map/ppermute | solution.py:56
  72.2 1.9 %collective-permute-start.32 = (bf16[160,1280]{1,0:T(8,128)(2,1)S(1)}, bf16[160,1280]{1,0:T(8,128)(2,1)S(1)}, u32[]{:S(2)}, u32[]{:S(2)}) collective-permute-start(bf16[160,1280]{1,0:T(8,128)(2,1)S(1)} %get-tuple-element.125), channel_id=1, source_target_pairs={{0,96},{1,97},{16,112},{17,113},{2,98},{3,99},{18,114},{19,115},{4... | collective-permute-start | bytes 1228808 | tf_op jit(solution)/shard_map/ppermute | solution.py:56
  74.1 8.6 %image_terms.1 = (f32[160,1152]{1,0:T(8,128)S(1)}, f32[160,1152]{1,0:T(8,128)S(1)}, bf16[160,1152]{1,0:T(8,128)(2,1)S(1)}, bf16[160,1152]{1,0:T(8,128)(2,1)S(1)}...) custom-call(bf16[1280,1280]{1,0:T(8,128)(2,1)S(1)} %get-tuple-elemen, ...), custom_call_target="tpu_custom_call" | custom-call | flops 10000000000 | bytes 11796480 | tf_op jit(solution)/shard_map/image_terms/pallas_call | solution.py:247
  82.9 2.0 %collective-permute-start.29 = (bf16[144,1280]{1,0:T(8,128)(2,1)S(1)}, bf16[144,1280]{1,0:T(8,128)(2,1)S(1)}, u32[]{:S(2)}, u32[]{:S(2)}) collective-permute-start(bf16[144,1280]{1,0:T(8,128)(2,1)S(1)} %add_rows.4), channel_id=1, source_target_pairs={{0,32},{1,33},{16,48},{17,49},{2,34},{3,35},{18,50},{19,51},{4,36}... | collective-permute-start | bytes 1105928 | tf_op jit(solution)/shard_map/ppermute | solution.py:56
  84.9 3.2 %collective-permute-start.25 = (bf16[160,1152]{1,0:T(8,128)(2,1)S(1)}, bf16[160,1152]{1,0:T(8,128)(2,1)S(1)}, u32[]{:S(2)}, u32[]{:S(2)}) collective-permute-start(bf16[160,1152]{1,0:T(8,128)(2,1)S(1)} %get-tuple-element.114), channel_id=1, source_target_pairs={{0,12},{1,13},{16,28},{17,29},{2,14},{3,15},{18,30},{19,31},{4,0},... | collective-permute-start | bytes 1105928 | tf_op jit(solution)/shard_map/ppermute | solution.py:56
  88.4 6.1 %collective-permute-done.25.refs_1_ = bf16[160,1152]{1,0:T(8,128)(2,1)S(1)} collective-permute-done((bf16[160,1152]{1,0:T(8,128)(2,1)S(1)}, bf16[160,1152]{1,0:T(8,128)(2,1)S(1)}, u32[]{:S(2)}, u32[]{:S(2)}) %collective-permute-start.25) | collective-permute-done | bytes 368672 | tf_op jit(solution)/shard_map/ppermute | solution.py:56
  94.7 3.8 %collective-permute-start.27 = (bf16[160,1152]{1,0:T(8,128)(2,1)S(1)}, bf16[160,1152]{1,0:T(8,128)(2,1)S(1)}, u32[]{:S(2)}, u32[]{:S(2)}) collective-permute-start(bf16[160,1152]{1,0:T(8,128)(2,1)S(1)} %add_rows.6), channel_id=1, source_target_pairs={{0,12},{1,13},{16,28},{17,29},{2,14},{3,15},{18,30},{19,31},{4,0},... | collective-permute-start | bytes 1105928 | tf_op jit(solution)/shard_map/ppermute | solution.py:56
  99.1 1.3 %collective-permute-start.34 = (bf16[160,1280]{1,0:T(8,128)(2,1)S(1)}, bf16[160,1280]{1,0:T(8,128)(2,1)S(1)}, u32[]{:S(2)}, u32[]{:S(2)}) collective-permute-start(bf16[160,1280]{1,0:T(8,128)(2,1)S(1)} %add_three.3.gave), channel_id=1, source_target_pairs={{0,16},{1,17},{16,0},{17,1},{2,18},{3,19},{18,2},{19,3},{4,20},{5,... | collective-permute-start | bytes 1228808 | tf_op jit(solution)/shard_map/ppermute | solution.py:56
  100.5 4.0 %collective-permute-done.26.ahead = bf16[160,1152]{1,0:T(8,128)(2,1)S(1)} collective-permute-done((bf16[160,1152]{1,0:T(8,128)(2,1)S(1)}, bf16[160,1152]{1,0:T(8,128)(2,1)S(1)}, u32[]{:S(2)}, u32[]{:S(2)}) %collective-permute-start.26) | collective-permute-done | bytes 368672 | tf_op jit(solution)/shard_map/ppermute | solution.py:56
  104.6 2.8 %collective-permute-start.28 = (bf16[160,1152]{1,0:T(8,128)(2,1)S(1)}, bf16[160,1152]{1,0:T(8,128)(2,1)S(1)}, u32[]{:S(2)}, u32[]{:S(2)}) collective-permute-start(bf16[160,1152]{1,0:T(8,128)(2,1)S(1)} %add_three.2), channel_id=1, source_target_pairs={{0,2},{1,3},{16,18},{17,19},{2,0},{3,1},{18,16},{19,17},{4,6},{5,7... | collective-permute-start | bytes 1105928 | tf_op jit(solution)/shard_map/ppermute | solution.py:56
  107.5 1.1 collective-permute-start.23
  108.6 2.1 %collective-permute-start.24 = (bf16[160,1152]{1,0:T(8,128)(2,1)S(1)}, bf16[160,1152]{1,0:T(8,128)(2,1)S(1)}, u32[]{:S(2)}, u32[]{:S(2)}) collective-permute-start(bf16[160,1152]{1,0:T(8,128)(2,1)S(1)} %get-tuple-element.111), channel_id=1, source_target_pairs={{0,12},{1,13},{16,28},{17,29},{2,14},{3,15},{18,30},{19,31},{4,0},... | collective-permute-start | bytes 1105928 | tf_op jit(solution)/shard_map/ppermute | solution.py:56
  111.8 4.9 %collective-permute-done.28.given = bf16[160,1152]{1,0:T(8,128)(2,1)S(1)} collective-permute-done((bf16[160,1152]{1,0:T(8,128)(2,1)S(1)}, bf16[160,1152]{1,0:T(8,128)(2,1)S(1)}, u32[]{:S(2)}, u32[]{:S(2)}) %collective-permute-start.28) | collective-permute-done | bytes 368672 | tf_op jit(solution)/shard_map/ppermute | solution.py:56
  116.7 1.1 image_final.1
  (72 shorter events, 10.8 us)
Async XLA Ops:
  0.6 10.8 %collective-permute-start.1 = (bf16[144,1280]{1,0:T(8,128)(2,1)}, bf16[144,1280]{1,0:T(8,128)(2,1)S(1)}, u32[]{:S(2)}, u32[]{:S(2)}) collective-permute-start(bf16[144,1280]{1,0:T(8,128)(2,1)} %bitcast.12), channel_id=1, source_target_pairs={{0,16},{1,17},{16,0},{17,1},{2,18},{3,19},{18,2},{19,3},{4,20},{5,... | collective-permute-start | bytes 1105928 | tf_op jit(solution)/shard_map/ppermute | solution.py:56
  2.6 17.3 %collective-permute-start.10 = (bf16[144,1280]{1,0:T(8,128)(2,1)}, bf16[144,1280]{1,0:T(8,128)(2,1)S(1)}, u32[]{:S(2)}, u32[]{:S(2)}) collective-permute-start(bf16[144,1280]{1,0:T(8,128)(2,1)} %bitcast.13), channel_id=1, source_target_pairs={{0,96},{1,97},{16,112},{17,113},{2,98},{3,99},{18,114},{19,115},{4... | collective-permute-start | bytes 1105928 | tf_op jit(solution)/shard_map/ppermute | solution.py:56
  5.3 20.9 %collective-permute-start.3 = (bf16[176,1152]{1,0:T(8,128)(2,1)S(1)}, bf16[176,1152]{1,0:T(8,128)(2,1)S(1)}, u32[]{:S(2)}, u32[]{:S(2)}) collective-permute-start(bf16[176,1152]{1,0:T(8,128)(2,1)S(1)} %get-tuple-element.66.value.refs_2_), channel_id=1, source_target_pairs={{0,12},{1,13},{16,28},{17,29},{2,14},{3,15},{18,30},{19,31},{4,0},... | collective-permute-start | bytes 1216520 | tf_op jit(solution)/shard_map/ppermute | solution.py:56
  8.4 11.5 %collective-permute-start = (bf16[176,1152]{1,0:T(8,128)(2,1)S(1)}, bf16[176,1152]{1,0:T(8,128)(2,1)S(1)}, u32[]{:S(2)}, u32[]{:S(2)}) collective-permute-start(bf16[176,1152]{1,0:T(8,128)(2,1)S(1)} %get-tuple-element.66.value.refs_2_), channel_id=1, source_target_pairs={{0,4},{1,5},{16,20},{17,21},{2,6},{3,7},{18,22},{19,23},{4,8},{5,9... | collective-permute-start | bytes 1216520 | tf_op jit(solution)/shard_map/ppermute | solution.py:56
  11.5 14.8 %collective-permute-start.2 = (bf16[176,1152]{1,0:T(8,128)(2,1)S(1)}, bf16[176,1152]{1,0:T(8,128)(2,1)S(1)}, u32[]{:S(2)}, u32[]{:S(2)}) collective-permute-start(bf16[176,1152]{1,0:T(8,128)(2,1)S(1)} %hold.1), channel_id=1, source_target_pairs={{0,2},{1,3},{16,18},{17,19},{2,0},{3,1},{18,16},{19,17},{4,6},{5,7... | collective-permute-start | bytes 1216520 | tf_op jit(solution)/shard_map/ppermute | solution.py:56
  15.2 9.3 %collective-permute-start.8 = (bf16[144,1280]{1,0:T(8,128)(2,1)S(1)}, bf16[144,1280]{1,0:T(8,128)(2,1)}, u32[]{:S(2)}, u32[]{:S(2)}) collective-permute-start(bf16[144,1280]{1,0:T(8,128)(2,1)S(1)} %bitcast.14), channel_id=1, source_target_pairs={{0,32},{1,33},{16,48},{17,49},{2,34},{3,35},{18,50},{19,51},{4,36}... | collective-permute-start | bytes 1105928 | tf_op jit(solution)/shard_map/ppermute | solution.py:56
  19.9 11.8 %collective-permute-start.4 = (bf16[176,1152]{1,0:T(8,128)(2,1)S(1)}, bf16[176,1152]{1,0:T(8,128)(2,1)S(1)}, u32[]{:S(2)}, u32[]{:S(2)}) collective-permute-start(bf16[176,1152]{1,0:T(8,128)(2,1)S(1)} %collective-permute-done.refs_3_), channel_id=1, source_target_pairs={{0,4},{1,5},{16,20},{17,21},{2,6},{3,7},{18,22},{19,23},{4,8},{5,9... | collective-permute-start | bytes 1216520 | tf_op jit(solution)/shard_map/ppermute | solution.py:56
  20.6 9.9 %collective-permute-start.11 = (bf16[144,1280]{1,0:T(8,128)(2,1)S(1)}, bf16[144,1280]{1,0:T(8,128)(2,1)}, u32[]{:S(2)}, u32[]{:S(2)}) collective-permute-start(bf16[144,1280]{1,0:T(8,128)(2,1)S(1)} %collective-permute-done.1.refs_0_.refs_1_), channel_id=1, source_target_pairs={{0,96},{1,97},{16,112},{17,113},{2,98},{3,99},{18,114},{19,115},{4... | collective-permute-start | bytes 1105928 | tf_op jit(solution)/shard_map/ppermute | solution.py:56
  24.5 10.5 %collective-permute-start.9 = (bf16[144,1280]{1,0:T(8,128)(2,1)S(1)}, bf16[144,1280]{1,0:T(8,128)(2,1)S(1)}, u32[]{:S(2)}, u32[]{:S(2)}) collective-permute-start(bf16[144,1280]{1,0:T(8,128)(2,1)S(1)} %collective-permute-done.1.refs_0_.refs_1_), channel_id=1, source_target_pairs={{0,32},{1,33},{16,48},{17,49},{2,34},{3,35},{18,50},{19,51},{4,36}... | collective-permute-start | bytes 1105928 | tf_op jit(solution)/shard_map/ppermute | solution.py:56
  26.2 12.9 %collective-permute-start.7 = (bf16[176,1152]{1,0:T(8,128)(2,1)S(1)}, bf16[176,1152]{1,0:T(8,128)(2,1)S(1)}, u32[]{:S(2)}, u32[]{:S(2)}) collective-permute-start(bf16[176,1152]{1,0:T(8,128)(2,1)S(1)} %collective-permute-done.2.refs_2_), channel_id=1, source_target_pairs={{0,12},{1,13},{16,28},{17,29},{2,14},{3,15},{18,30},{19,31},{4,0},... | collective-permute-start | bytes 1216520 | tf_op jit(solution)/shard_map/ppermute | solution.py:56
  29.2 9.9 %collective-permute-start.6 = (bf16[176,1152]{1,0:T(8,128)(2,1)S(1)}, bf16[176,1152]{1,0:T(8,128)(2,1)S(1)}, u32[]{:S(2)}, u32[]{:S(2)}) collective-permute-start(bf16[176,1152]{1,0:T(8,128)(2,1)S(1)} %collective-permute-done.2.refs_2_), channel_id=1, source_target_pairs={{0,4},{1,5},{16,20},{17,21},{2,6},{3,7},{18,22},{19,23},{4,8},{5,9... | collective-permute-start | bytes 1216520 | tf_op jit(solution)/shard_map/ppermute | solution.py:56
  30.5 10.9 %collective-permute-start.14 = (bf16[144,1280]{1,0:T(8,128)(2,1)}, bf16[144,1280]{1,0:T(8,128)(2,1)S(1)}, u32[]{:S(2)}, u32[]{:S(2)}) collective-permute-start(bf16[144,1280]{1,0:T(8,128)(2,1)} %collective-permute-done.8.refs_2_), channel_id=1, source_target_pairs={{0,32},{1,33},{16,48},{17,49},{2,34},{3,35},{18,50},{19,51},{4,36}... | collective-permute-start | bytes 1105928 | tf_op jit(solution)/shard_map/ppermute | solution.py:56
  31.7 9.8 %collective-permute-start.15 = (bf16[144,1280]{1,0:T(8,128)(2,1)}, bf16[144,1280]{1,0:T(8,128)(2,1)S(1)}, u32[]{:S(2)}, u32[]{:S(2)}) collective-permute-start(bf16[144,1280]{1,0:T(8,128)(2,1)} %collective-permute-done.11.refs_5_), channel_id=1, source_target_pairs={{0,96},{1,97},{16,112},{17,113},{2,98},{3,99},{18,114},{19,115},{4... | collective-permute-start | bytes 1105928 | tf_op jit(solution)/shard_map/ppermute | solution.py:56
  35.0 12.6 %collective-permute-start.5 = (bf16[704,1152]{1,0:T(8,128)(2,1)S(1)}, bf16[704,1152]{1,0:T(8,128)(2,1)S(1)}, u32[]{:S(2)}, u32[]{:S(2)}) collective-permute-start(bf16[704,1152]{1,0:T(8,128)(2,1)S(1)} %pad_maximum_fusion), channel_id=1, source_target_pairs={{0,1},{1,0},{16,17},{17,16},{2,3},{3,2},{18,19},{19,18},{4,5},{5,4... | collective-permute-start | bytes 4866056 | tf_op jit(solution)/shard_map/ppermute | solution.py:56
  41.5 11.8 %collective-permute-start.17 = (bf16[528,1152]{1,0:T(8,128)(2,1)S(1)}, bf16[528,1152]{1,0:T(8,128)(2,1)S(1)}, u32[]{:S(2)}, u32[]{:S(2)}) collective-permute-start(bf16[528,1152]{1,0:T(8,128)(2,1)S(1)} %pad_maximum_fusion.1), channel_id=1, source_target_pairs={{0,1},{1,0},{16,17},{17,16},{2,3},{3,2},{18,19},{19,18},{4,5},{5,4... | collective-permute-start | bytes 3649544 | tf_op jit(solution)/shard_map/ppermute | solution.py:56
  58.8 15.3 %collective-permute-start.20 = (bf16[1152,1280]{1,0:T(8,128)(2,1)S(1)}, bf16[1152,1280]{1,0:T(8,128)(2,1)S(1)}, u32[]{:S(2)}, u32[]{:S(2)}) collective-permute-start(bf16[1152,1280]{1,0:T(8,128)(2,1)S(1)} %get-tuple-element.96.refs_7_.refs_9_.refs_4_), channel_id=1, source_target_pairs={{0,1},{1,0},{16,17},{17,16},{2,3},{3,2},{18,19},{19,18},{4,5},{5,4... | collective-permute-start | bytes 8847368 | tf_op jit(solution)/shard_map/ppermute | solution.py:56
  59.4 9.2 %collective-permute-start.19 = (bf16[640,1280]{1,0:T(8,128)(2,1)S(1)}, bf16[640,1280]{1,0:T(8,128)(2,1)S(1)}, u32[]{:S(2)}, u32[]{:S(2)}) collective-permute-start(bf16[640,1280]{1,0:T(8,128)(2,1)S(1)} %get-tuple-element.83), channel_id=1, source_target_pairs={{0,1},{1,0},{16,17},{17,16},{2,3},{3,2},{18,19},{19,18},{4,5},{5,4... | collective-permute-start | bytes 4915208 | tf_op jit(solution)/shard_map/ppermute | solution.py:56
  59.5 14.6 %collective-permute-start.16 = (bf16[640,1280]{1,0:T(8,128)(2,1)S(1)}, bf16[640,1280]{1,0:T(8,128)(2,1)S(1)}, u32[]{:S(2)}, u32[]{:S(2)}) collective-permute-start(bf16[640,1280]{1,0:T(8,128)(2,1)S(1)} %get-tuple-element.80), channel_id=1, source_target_pairs={{0,1},{1,0},{16,17},{17,16},{2,3},{3,2},{18,19},{19,18},{4,5},{5,4... | collective-permute-start | bytes 4915208 | tf_op jit(solution)/shard_map/ppermute | solution.py:56
  68.6 14.2 %collective-permute-start.21 = (bf16[144,1280]{1,0:T(8,128)(2,1)S(1)}, bf16[144,1280]{1,0:T(8,128)(2,1)S(1)}, u32[]{:S(2)}, u32[]{:S(2)}) collective-permute-start(bf16[144,1280]{1,0:T(8,128)(2,1)S(1)} %get-tuple-element.102), channel_id=1, source_target_pairs={{0,32},{1,33},{16,48},{17,49},{2,34},{3,35},{18,50},{19,51},{4,36}... | collective-permute-start | bytes 1105928 | tf_op jit(solution)/shard_map/ppermute | solution.py:56
  72.1 22.6 %collective-permute-start.31 = (bf16[160,1280]{1,0:T(8,128)(2,1)S(1)}, bf16[160,1280]{1,0:T(8,128)(2,1)S(1)}, u32[]{:S(2)}, u32[]{:S(2)}) collective-permute-start(bf16[160,1280]{1,0:T(8,128)(2,1)S(1)} %get-tuple-element.123), channel_id=1, source_target_pairs={{0,32},{1,33},{16,48},{17,49},{2,34},{3,35},{18,50},{19,51},{4,36}... | collective-permute-start | bytes 1228808 | tf_op jit(solution)/shard_map/ppermute | solution.py:56
  72.2 16.0 %collective-permute-start.32 = (bf16[160,1280]{1,0:T(8,128)(2,1)S(1)}, bf16[160,1280]{1,0:T(8,128)(2,1)S(1)}, u32[]{:S(2)}, u32[]{:S(2)}) collective-permute-start(bf16[160,1280]{1,0:T(8,128)(2,1)S(1)} %get-tuple-element.125), channel_id=1, source_target_pairs={{0,96},{1,97},{16,112},{17,113},{2,98},{3,99},{18,114},{19,115},{4... | collective-permute-start | bytes 1228808 | tf_op jit(solution)/shard_map/ppermute | solution.py:56
  82.9 25.7 %collective-permute-start.29 = (bf16[144,1280]{1,0:T(8,128)(2,1)S(1)}, bf16[144,1280]{1,0:T(8,128)(2,1)S(1)}, u32[]{:S(2)}, u32[]{:S(2)}) collective-permute-start(bf16[144,1280]{1,0:T(8,128)(2,1)S(1)} %add_rows.4), channel_id=1, source_target_pairs={{0,32},{1,33},{16,48},{17,49},{2,34},{3,35},{18,50},{19,51},{4,36}... | collective-permute-start | bytes 1105928 | tf_op jit(solution)/shard_map/ppermute | solution.py:56
  84.9 15.5 %collective-permute-start.22 = (bf16[160,1152]{1,0:T(8,128)(2,1)S(1)}, bf16[160,1152]{1,0:T(8,128)(2,1)S(1)}, u32[]{:S(2)}, u32[]{:S(2)}) collective-permute-start(bf16[160,1152]{1,0:T(8,128)(2,1)S(1)} %get-tuple-element.108), channel_id=1, source_target_pairs={{0,4},{1,5},{16,20},{17,21},{2,6},{3,7},{18,22},{19,23},{4,8},{5,9... | collective-permute-start | bytes 1105928 | tf_op jit(solution)/shard_map/ppermute | solution.py:56
  84.9 9.6 %collective-permute-start.25 = (bf16[160,1152]{1,0:T(8,128)(2,1)S(1)}, bf16[160,1152]{1,0:T(8,128)(2,1)S(1)}, u32[]{:S(2)}, u32[]{:S(2)}) collective-permute-start(bf16[160,1152]{1,0:T(8,128)(2,1)S(1)} %get-tuple-element.114), channel_id=1, source_target_pairs={{0,12},{1,13},{16,28},{17,29},{2,14},{3,15},{18,30},{19,31},{4,0},... | collective-permute-start | bytes 1105928 | tf_op jit(solution)/shard_map/ppermute | solution.py:56
  88.2 10.7 %collective-permute-start.33 = (bf16[160,1280]{1,0:T(8,128)(2,1)S(1)}, bf16[160,1280]{1,0:T(8,128)(2,1)S(1)}, u32[]{:S(2)}, u32[]{:S(2)}) collective-permute-start(bf16[160,1280]{1,0:T(8,128)(2,1)S(1)} %add_rows.7), channel_id=1, source_target_pairs={{0,96},{1,97},{16,112},{17,113},{2,98},{3,99},{18,114},{19,115},{4... | collective-permute-start | bytes 1228808 | tf_op jit(solution)/shard_map/ppermute | solution.py:56
  94.6 9.9 %collective-permute-start.26 = (bf16[160,1152]{1,0:T(8,128)(2,1)S(1)}, bf16[160,1152]{1,0:T(8,128)(2,1)S(1)}, u32[]{:S(2)}, u32[]{:S(2)}) collective-permute-start(bf16[160,1152]{1,0:T(8,128)(2,1)S(1)} %get-tuple-element.117), channel_id=1, source_target_pairs={{0,4},{1,5},{16,20},{17,21},{2,6},{3,7},{18,22},{19,23},{4,8},{5,9... | collective-permute-start | bytes 1105928 | tf_op jit(solution)/shard_map/ppermute | solution.py:56
  94.7 9.8 %collective-permute-start.27 = (bf16[160,1152]{1,0:T(8,128)(2,1)S(1)}, bf16[160,1152]{1,0:T(8,128)(2,1)S(1)}, u32[]{:S(2)}, u32[]{:S(2)}) collective-permute-start(bf16[160,1152]{1,0:T(8,128)(2,1)S(1)} %add_rows.6), channel_id=1, source_target_pairs={{0,12},{1,13},{16,28},{17,29},{2,14},{3,15},{18,30},{19,31},{4,0},... | collective-permute-start | bytes 1105928 | tf_op jit(solution)/shard_map/ppermute | solution.py:56
  99.1 11.6 %collective-permute-start.34 = (bf16[160,1280]{1,0:T(8,128)(2,1)S(1)}, bf16[160,1280]{1,0:T(8,128)(2,1)S(1)}, u32[]{:S(2)}, u32[]{:S(2)}) collective-permute-start(bf16[160,1280]{1,0:T(8,128)(2,1)S(1)} %add_three.3.gave), channel_id=1, source_target_pairs={{0,16},{1,17},{16,0},{17,1},{2,18},{3,19},{18,2},{19,3},{4,20},{5,... | collective-permute-start | bytes 1228808 | tf_op jit(solution)/shard_map/ppermute | solution.py:56
  100.4 10.2 %collective-permute-start.30 = (bf16[144,1280]{1,0:T(8,128)(2,1)S(1)}, bf16[144,1280]{1,0:T(8,128)(2,1)S(1)}, u32[]{:S(2)}, u32[]{:S(2)}) collective-permute-start(bf16[144,1280]{1,0:T(8,128)(2,1)S(1)} %get-tuple-element.121), channel_id=1, source_target_pairs={{0,96},{1,97},{16,112},{17,113},{2,98},{3,99},{18,114},{19,115},{4... | collective-permute-start | bytes 1105928 | tf_op jit(solution)/shard_map/ppermute | solution.py:56
  104.6 12.0 %collective-permute-start.28 = (bf16[160,1152]{1,0:T(8,128)(2,1)S(1)}, bf16[160,1152]{1,0:T(8,128)(2,1)S(1)}, u32[]{:S(2)}, u32[]{:S(2)}) collective-permute-start(bf16[160,1152]{1,0:T(8,128)(2,1)S(1)} %add_three.2), channel_id=1, source_target_pairs={{0,2},{1,3},{16,18},{17,19},{2,0},{3,1},{18,16},{19,17},{4,6},{5,7... | collective-permute-start | bytes 1105928 | tf_op jit(solution)/shard_map/ppermute | solution.py:56
  107.5 9.2 %collective-permute-start.23 = (bf16[160,1152]{1,0:T(8,128)(2,1)S(1)}, bf16[160,1152]{1,0:T(8,128)(2,1)S(1)}, u32[]{:S(2)}, u32[]{:S(2)}) collective-permute-start(bf16[160,1152]{1,0:T(8,128)(2,1)S(1)} %add_rows.5), channel_id=1, source_target_pairs={{0,4},{1,5},{16,20},{17,21},{2,6},{3,7},{18,22},{19,23},{4,8},{5,9... | collective-permute-start | bytes 1105928 | tf_op jit(solution)/shard_map/ppermute | solution.py:56
  108.6 8.1 %collective-permute-start.24 = (bf16[160,1152]{1,0:T(8,128)(2,1)S(1)}, bf16[160,1152]{1,0:T(8,128)(2,1)S(1)}, u32[]{:S(2)}, u32[]{:S(2)}) collective-permute-start(bf16[160,1152]{1,0:T(8,128)(2,1)S(1)} %get-tuple-element.111), channel_id=1, source_target_pairs={{0,12},{1,13},{16,28},{17,29},{2,14},{3,15},{18,30},{19,31},{4,0},... | collective-permute-start | bytes 1105928 | tf_op jit(solution)/shard_map/ppermute | solution.py:56
  (9 other events, 52.9 us)
